TPU v7x, 1024 devices: a whole 4x4x32 slice. The times are simulated.
1024 devices in a mesh: occ: 8 (over x, core), vir: 128 (over y, z).
Axes of the slice: x: 4, y: 4, z: 32, core: 2. Of those that a mesh axis runs over, the one named last changes fastest.
Arguments:
- amps: bfloat16 [2048, 65536], P('occ', 'vir'), may hold values from -6 to 6
- integrals: bfloat16 [128, 5, 512, 512], P('vir'), may hold values from -0.25 to 0.25
- mask: int32 [128, 5], P('vir'), may hold values 0 or 1
- pair_coupling: bfloat16 [2048, 2048], P('occ'), may hold values from -0.125 to 0.125
- occ_energy: float32 [2048], P('occ'), may hold values from -2 to -0.5
- vir_energy: float32 [65536], P('vir'), may hold values from 0.5 to 4
Outputs:
- update: float32 [2048, 65536], P('occ', 'vir')
All inputs are finite; a program needn't handle non-finite values. No bound on the sum of `mask` on one device may be relied on, other than what follows from the above.
Results may differ from a plain program's by a relative error of at most 0.0003.
Values may be sent and summed in bfloat16 or wider, within the bound.
No kernel may reach another device: no remote copies, remote signals or barrier semaphores. Data moves between devices by JAX's collectives and lax.ppermute only.
A program may use at most 32 MiB of HBM per device.

v0:
```python
import jax
import jax.numpy as jnp
from jax import lax
from jax.sharding import PartitionSpec as P


def shifted(block, axis, distance):
    devices = range(lax.axis_size(axis))
    route = [(i - distance, i) for i in devices if i - distance in devices]
    return lax.ppermute(block, axis, route)


def block_term(left, block, flag):
    return jnp.dot(left, block, preferred_element_type=jnp.float32) * flag.astype(jnp.float32)


def body(amps, integrals, mask, pair_coupling, occ_energy, vir_energy):
    blocks = integrals.shape[1]
    reach = (blocks - 1) // 2
    total = jnp.dot(
        pair_coupling,
        lax.all_gather(amps, "occ", axis=0, tiled=True),
        preferred_element_type=jnp.float32,
    )
    total = total + block_term(amps, integrals[0, reach], mask[0, reach])
    for k in range(blocks):
        if k == reach:
            continue
        offset = reach - k
        far_tile, far_block, far_flag = shifted(
            (amps, integrals[0, k], mask[0, k : k + 1]), "vir", offset
        )
        total = total + block_term(far_tile, far_block, far_flag[0])
    return total / (occ_energy[:, None] - vir_energy[None, :])


def solution(mesh):
    placed = (
        P("occ", "vir"),
        P("vir", None, None, None),
        P("vir", None),
        P("occ", None),
        P("occ"),
        P("vir"),
    )
    return jax.shard_map(
        body, mesh=mesh, in_specs=placed, out_specs=P("occ", "vir"), check_vma=False
    )
```

profile of v0, /device:TPU:24, one launch (start us, length us, event | category | flops | bytes accessed | tf_op | source)
XLA Modules:
  0.0 131.1 jit_solution(10916951921522192804)
XLA Ops:
  6.5 0.7 all-gather.2.cloned.1.call-update
  7.3 2.4 %slice_bitcast_fusion.3 = (bf16[512,512]{1,0:T(8,128)(2,1)}, bf16[512,512]{1,0:T(8,128)(2,1)S(1)}, bf16[512,512]{1,0:T(8,128)(2,1)S(1)}, bf16[512,512]{1,0:T(8,128)(2,1)S(1)}) fusion(bf16[1,5,512,512]{3,2,1,0:T(8,128)(2,1)} %param.7), kind=kLoop, calls=%fused_computation.15 | loop fusion | bytes 4194304 | tf_op jit(solution)/shard_map/squeeze | solution.py:31
  9.7 3.8 %collective-permute-start.4 = (bf16[512,512]{1,0:T(8,128)(2,1)S(1)}, bf16[512,512]{1,0:T(8,128)(2,1)S(1)}, u32[]{:S(2)}, u32[]{:S(2)}) collective-permute-start(bf16[512,512]{1,0:T(8,128)(2,1)S(1)} %get-tuple-element.6), channel_id=1, source_target_pairs={{0,1},{1,2},{2,3},{3,4},{4,5},{5,6},{6,7},{7,8},{8,9},{9,10},{10,1... | collective-permute-start | bytes 1572872 | tf_op jit(solution)/shard_map/ppermute | solution.py:10
  13.5 3.8 %collective-permute-start.3 = (bf16[256,512]{1,0:T(8,128)(2,1)S(1)}, bf16[256,512]{1,0:T(8,128)(2,1)S(1)}, u32[]{:S(2)}, u32[]{:S(2)}) collective-permute-start(bf16[256,512]{1,0:T(8,128)(2,1)S(1)} %copy-done.1), channel_id=1, source_target_pairs={{0,1},{1,2},{2,3},{3,4},{4,5},{5,6},{6,7},{7,8},{8,9},{9,10},{10,1... | collective-permute-start | bytes 786440 | tf_op jit(solution)/shard_map/ppermute | solution.py:10
  17.4 16.5 %collective-permute-start.9 = (bf16[256,512]{1,0:T(8,128)(2,1)S(1)}, bf16[256,512]{1,0:T(8,128)(2,1)S(1)}, u32[]{:S(2)}, u32[]{:S(2)}) collective-permute-start(bf16[256,512]{1,0:T(8,128)(2,1)S(1)} %copy-done.1), channel_id=1, source_target_pairs={{2,0},{3,1},{4,2},{5,3},{6,4},{7,5},{8,6},{9,7},{10,8},{11,9},{12,... | collective-permute-start | bytes 786440 | tf_op jit(solution)/shard_map/ppermute | solution.py:10
  33.9 4.4 %collective-permute-start.10 = (bf16[512,512]{1,0:T(8,128)(2,1)S(1)}, bf16[512,512]{1,0:T(8,128)(2,1)S(1)}, u32[]{:S(2)}, u32[]{:S(2)}) collective-permute-start(bf16[512,512]{1,0:T(8,128)(2,1)S(1)} %get-tuple-element.7), channel_id=1, source_target_pairs={{2,0},{3,1},{4,2},{5,3},{6,4},{7,5},{8,6},{9,7},{10,8},{11,9},{12,... | collective-permute-start | bytes 1572872 | tf_op jit(solution)/shard_map/ppermute | solution.py:10
  38.3 0.7 fusion.7
  38.9 2.4 %collective-permute-start.2 = (s32[1]{0:T(128)}, s32[1]{0:T(128)}, u32[]{:S(2)}, u32[]{:S(2)}) collective-permute-start(s32[1]{0:T(128)} %bitcast.3), channel_id=1, source_target_pairs={{0,2},{1,3},{2,4},{3,5},{4,6},{5,7},{6,8},{7,9},{8,10},{9,11},{10,... | collective-permute-start | bytes 20 | tf_op jit(solution)/shard_map/ppermute | solution.py:10
  41.9 5.6 %collective-permute-done.2 = s32[1]{0:T(128)} collective-permute-done((s32[1]{0:T(128)}, s32[1]{0:T(128)}, u32[]{:S(2)}, u32[]{:S(2)}) %collective-permute-start.2) | collective-permute-done | bytes 36 | tf_op jit(solution)/shard_map/ppermute | solution.py:10
  47.5 2.9 %collective-permute-start.5 = (s32[1]{0:T(128)}, s32[1]{0:T(128)}, u32[]{:S(2)}, u32[]{:S(2)}) collective-permute-start(s32[1]{0:T(128)} %bitcast.6), channel_id=1, source_target_pairs={{0,1},{1,2},{2,3},{3,4},{4,5},{5,6},{6,7},{7,8},{8,9},{9,10},{10,1... | collective-permute-start | bytes 20 | tf_op jit(solution)/shard_map/ppermute | solution.py:10
  50.5 4.8 %collective-permute-done.5 = s32[1]{0:T(128)} collective-permute-done((s32[1]{0:T(128)}, s32[1]{0:T(128)}, u32[]{:S(2)}, u32[]{:S(2)}) %collective-permute-start.5) | collective-permute-done | bytes 36 | tf_op jit(solution)/shard_map/ppermute | solution.py:10
  55.2 1.9 %collective-permute-start.11 = (s32[1]{0:T(128)}, s32[1]{0:T(128)}, u32[]{:S(2)}, u32[]{:S(2)}) collective-permute-start(s32[1]{0:T(128)} %bitcast.12), channel_id=1, source_target_pairs={{2,0},{3,1},{4,2},{5,3},{6,4},{7,5},{8,6},{9,7},{10,8},{11,9},{12,... | collective-permute-start | bytes 20 | tf_op jit(solution)/shard_map/ppermute | solution.py:10
  57.2 10.1 %collective-permute-done.11 = s32[1]{0:T(128)} collective-permute-done((s32[1]{0:T(128)}, s32[1]{0:T(128)}, u32[]{:S(2)}, u32[]{:S(2)}) %collective-permute-start.11) | collective-permute-done | bytes 36 | tf_op jit(solution)/shard_map/ppermute | solution.py:10
  67.3 1.9 %collective-permute-start.8 = (s32[1]{0:T(128)}, s32[1]{0:T(128)}, u32[]{:S(2)}, u32[]{:S(2)}) collective-permute-start(s32[1]{0:T(128)} %bitcast.9), channel_id=1, source_target_pairs={{1,0},{2,1},{3,2},{4,3},{5,4},{6,5},{7,6},{8,7},{9,8},{10,9},{11,1... | collective-permute-start | bytes 20 | tf_op jit(solution)/shard_map/ppermute | solution.py:10
  69.2 3.7 %collective-permute-done.8 = s32[1]{0:T(128)} collective-permute-done((s32[1]{0:T(128)}, s32[1]{0:T(128)}, u32[]{:S(2)}, u32[]{:S(2)}) %collective-permute-start.8) | collective-permute-done | bytes 36 | tf_op jit(solution)/shard_map/ppermute | solution.py:10
  72.9 5.7 %collective-permute-start.7 = (bf16[512,512]{1,0:T(8,128)(2,1)S(1)}, bf16[512,512]{1,0:T(8,128)(2,1)S(1)}, u32[]{:S(2)}, u32[]{:S(2)}) collective-permute-start(bf16[512,512]{1,0:T(8,128)(2,1)S(1)} %get-tuple-element.8), channel_id=1, source_target_pairs={{1,0},{2,1},{3,2},{4,3},{5,4},{6,5},{7,6},{8,7},{9,8},{10,9},{11,1... | collective-permute-start | bytes 1572872 | tf_op jit(solution)/shard_map/ppermute | solution.py:10
  78.6 1.3 %convolution_multiply_fusion.4 = f32[256,512]{1,0:T(8,128)S(1)} fusion(bf16[256,512]{1,0:T(8,128)(2,1)S(1)} %copy-done.1, bf16[1,5,512,512]{3,2,1,0:T(8,128)(2,1)} %param.7, f32[]{:T(128)} %bitcast.1), kind=kOutput, calls=%fused_computation.10 | convolution fusion | flops 134348800 | bytes 1311232 | tf_op jit(solution)/shard_map/dot_general | solution.py:14
  82.5 0.0 collective-permute-done.3
  82.5 1.9 %collective-permute-start = (bf16[256,512]{1,0:T(8,128)(2,1)S(1)}, bf16[256,512]{1,0:T(8,128)(2,1)}, u32[]{:S(2)}, u32[]{:S(2)}) collective-permute-start(bf16[256,512]{1,0:T(8,128)(2,1)S(1)} %copy-done.1), channel_id=1, source_target_pairs={{0,2},{1,3},{2,4},{3,5},{4,6},{5,7},{6,8},{7,9},{8,10},{9,11},{10,... | collective-permute-start | bytes 786440 | tf_op jit(solution)/shard_map/ppermute | solution.py:10
  84.4 0.0 collective-permute-done.4
  84.5 4.1 %collective-permute-start.6 = (bf16[256,512]{1,0:T(8,128)(2,1)S(1)}, bf16[256,512]{1,0:T(8,128)(2,1)S(1)}, u32[]{:S(2)}, u32[]{:S(2)}) collective-permute-start(bf16[256,512]{1,0:T(8,128)(2,1)S(1)} %copy-done.1), channel_id=1, source_target_pairs={{1,0},{2,1},{3,2},{4,3},{5,4},{6,5},{7,6},{8,7},{9,8},{10,9},{11,1... | collective-permute-start | bytes 786440 | tf_op jit(solution)/shard_map/ppermute | solution.py:10
  88.6 0.3 convolution_multiply_fusion.2
  88.9 0.0 collective-permute-done.9
  88.9 1.9 %collective-permute-start.1 = (bf16[512,512]{1,0:T(8,128)(2,1)}, bf16[512,512]{1,0:T(8,128)(2,1)}, u32[]{:S(2)}, u32[]{:S(2)}) collective-permute-start(bf16[512,512]{1,0:T(8,128)(2,1)} %get-tuple-element.5), channel_id=1, source_target_pairs={{0,2},{1,3},{2,4},{3,5},{4,6},{5,7},{6,8},{7,9},{8,10},{9,11},{10,... | collective-permute-start | bytes 1572872 | tf_op jit(solution)/shard_map/ppermute | solution.py:10
  90.8 0.3 convolution_multiply_fusion
  91.1 2.7 %collective-permute-done.6 = bf16[256,512]{1,0:T(8,128)(2,1)S(1)} collective-permute-done((bf16[256,512]{1,0:T(8,128)(2,1)S(1)}, bf16[256,512]{1,0:T(8,128)(2,1)S(1)}, u32[]{:S(2)}, u32[]{:S(2)}) %collective-permute-start.6) | collective-permute-done | bytes 262176 | tf_op jit(solution)/shard_map/ppermute | solution.py:10
  93.9 0.3 convolution_multiply_fusion.1
  94.2 0.0 all-gather.2.cloned.1.call-done
  94.2 2.3 %convolution_add_fusion = f32[256,512]{1,0:T(8,128)S(1)} fusion(f32[256,512]{1,0:T(8,128)S(1)} %convolution_multiply_fusion.4, bf16[256,2048]{1,0:T(8,128)(2,1)S(1)} %copy-done, bf16[2048,512]{1,0:T(8,128)(2,1)} %all-gather.2.cloned.1.call-done), kind=kOutput, calls=%fused_computation | convolution fusion | flops 537001984 | bytes 4194304 | tf_op jit(solution)/shard_map/dot_general | solution.py:20
  96.5 9.1 %collective-permute-done = bf16[256,512]{1,0:T(8,128)(2,1)} collective-permute-done((bf16[256,512]{1,0:T(8,128)(2,1)S(1)}, bf16[256,512]{1,0:T(8,128)(2,1)}, u32[]{:S(2)}, u32[]{:S(2)}) %collective-permute-start) | collective-permute-done | bytes 262176 | tf_op jit(solution)/shard_map/ppermute | solution.py:10
  105.6 16.3 %collective-permute-done.1 = bf16[512,512]{1,0:T(8,128)(2,1)} collective-permute-done((bf16[512,512]{1,0:T(8,128)(2,1)}, bf16[512,512]{1,0:T(8,128)(2,1)}, u32[]{:S(2)}, u32[]{:S(2)}) %collective-permute-start.1) | collective-permute-done | bytes 524320 | tf_op jit(solution)/shard_map/ppermute | solution.py:10
  122.0 2.3 %fusion.4 = f32[256,512]{1,0:T(8,128)} fusion(f32[256,512]{1,0:T(8,128)S(1)} %convolution_multiply_fusion, f32[256,512]{1,0:T(8,128)S(1)} %convolution_multiply_fusion.1, f32[256,512]{1,0:T(8,128)S(1)} %convolution_multiply_fusion.2, f32[256,512]{1,0:T(8,128)S(1)} %convolution_add_fusion, bf16[256,512]{1,0:T(8,128)(2,1)} %collective-permute-done, ...), kind=kOutput, calls=%fused_computation.9 | convolution fusion | flops 135135232 | bytes 3410948 | tf_op jit(solution)/shard_map/dot_general | solution.py:14
  (13 shorter events, 0.0 us)
Async XLA Ops:
  6.5 87.7 %copy-start = (bf16[256,2048]{1,0:T(8,128)(2,1)S(1)}, bf16[256,2048]{1,0:T(8,128)(2,1)}, u32[]{:S(2)}) copy-start(bf16[256,2048]{1,0:T(8,128)(2,1)} %param.9) | copy-start | bytes 3145732
  6.5 7.0 %copy-start.1 = (bf16[256,512]{1,0:T(8,128)(2,1)S(1)}, bf16[256,512]{1,0:T(8,128)(2,1)}, u32[]{:S(2)}) copy-start(bf16[256,512]{1,0:T(8,128)(2,1)} %param.6) | copy-start | bytes 786436
  6.5 31.7 %copy-start.2 = (s32[1,5]{1,0:T(1,128)S(1)}, s32[1,5]{1,0:T(1,128)}, u32[]{:S(2)}) copy-start(s32[1,5]{1,0:T(1,128)} %param.8) | copy-start | bytes 64
  6.5 87.7 %all-gather.2.cloned.1.call-start = ((), (), s32[]{:S(2)}) async-start(), calls=%async_computation | async-start | bytes 2359296 | tf_op jit(solution)/shard_map/all_gather | solution.py:22
  9.7 74.7 %collective-permute-start.4 = (bf16[512,512]{1,0:T(8,128)(2,1)S(1)}, bf16[512,512]{1,0:T(8,128)(2,1)S(1)}, u32[]{:S(2)}, u32[]{:S(2)}) collective-permute-start(bf16[512,512]{1,0:T(8,128)(2,1)S(1)} %get-tuple-element.6), channel_id=1, source_target_pairs={{0,1},{1,2},{2,3},{3,4},{4,5},{5,6},{6,7},{7,8},{8,9},{9,10},{10,1... | collective-permute-start | bytes 1572872 | tf_op jit(solution)/shard_map/ppermute | solution.py:10
  13.5 69.0 %collective-permute-start.3 = (bf16[256,512]{1,0:T(8,128)(2,1)S(1)}, bf16[256,512]{1,0:T(8,128)(2,1)S(1)}, u32[]{:S(2)}, u32[]{:S(2)}) collective-permute-start(bf16[256,512]{1,0:T(8,128)(2,1)S(1)} %copy-done.1), channel_id=1, source_target_pairs={{0,1},{1,2},{2,3},{3,4},{4,5},{5,6},{6,7},{7,8},{8,9},{9,10},{10,1... | collective-permute-start | bytes 786440 | tf_op jit(solution)/shard_map/ppermute | solution.py:10
  17.4 71.5 %collective-permute-start.9 = (bf16[256,512]{1,0:T(8,128)(2,1)S(1)}, bf16[256,512]{1,0:T(8,128)(2,1)S(1)}, u32[]{:S(2)}, u32[]{:S(2)}) collective-permute-start(bf16[256,512]{1,0:T(8,128)(2,1)S(1)} %copy-done.1), channel_id=1, source_target_pairs={{2,0},{3,1},{4,2},{5,3},{6,4},{7,5},{8,6},{9,7},{10,8},{11,9},{12,... | collective-permute-start | bytes 786440 | tf_op jit(solution)/shard_map/ppermute | solution.py:10
  33.9 56.9 %collective-permute-start.10 = (bf16[512,512]{1,0:T(8,128)(2,1)S(1)}, bf16[512,512]{1,0:T(8,128)(2,1)S(1)}, u32[]{:S(2)}, u32[]{:S(2)}) collective-permute-start(bf16[512,512]{1,0:T(8,128)(2,1)S(1)} %get-tuple-element.7), channel_id=1, source_target_pairs={{2,0},{3,1},{4,2},{5,3},{6,4},{7,5},{8,6},{9,7},{10,8},{11,9},{12,... | collective-permute-start | bytes 1572872 | tf_op jit(solution)/shard_map/ppermute | solution.py:10
  38.9 8.6 %collective-permute-start.2 = (s32[1]{0:T(128)}, s32[1]{0:T(128)}, u32[]{:S(2)}, u32[]{:S(2)}) collective-permute-start(s32[1]{0:T(128)} %bitcast.3), channel_id=1, source_target_pairs={{0,2},{1,3},{2,4},{3,5},{4,6},{5,7},{6,8},{7,9},{8,10},{9,11},{10,... | collective-permute-start | bytes 20 | tf_op jit(solution)/shard_map/ppermute | solution.py:10
  47.5 7.7 %collective-permute-start.5 = (s32[1]{0:T(128)}, s32[1]{0:T(128)}, u32[]{:S(2)}, u32[]{:S(2)}) collective-permute-start(s32[1]{0:T(128)} %bitcast.6), channel_id=1, source_target_pairs={{0,1},{1,2},{2,3},{3,4},{4,5},{5,6},{6,7},{7,8},{8,9},{9,10},{10,1... | collective-permute-start | bytes 20 | tf_op jit(solution)/shard_map/ppermute | solution.py:10
  55.2 12.0 %collective-permute-start.11 = (s32[1]{0:T(128)}, s32[1]{0:T(128)}, u32[]{:S(2)}, u32[]{:S(2)}) collective-permute-start(s32[1]{0:T(128)} %bitcast.12), channel_id=1, source_target_pairs={{2,0},{3,1},{4,2},{5,3},{6,4},{7,5},{8,6},{9,7},{10,8},{11,9},{12,... | collective-permute-start | bytes 20 | tf_op jit(solution)/shard_map/ppermute | solution.py:10
  67.3 5.6 %collective-permute-start.8 = (s32[1]{0:T(128)}, s32[1]{0:T(128)}, u32[]{:S(2)}, u32[]{:S(2)}) collective-permute-start(s32[1]{0:T(128)} %bitcast.9), channel_id=1, source_target_pairs={{1,0},{2,1},{3,2},{4,3},{5,4},{6,5},{7,6},{8,7},{9,8},{10,9},{11,1... | collective-permute-start | bytes 20 | tf_op jit(solution)/shard_map/ppermute | solution.py:10
  72.9 21.0 %collective-permute-start.7 = (bf16[512,512]{1,0:T(8,128)(2,1)S(1)}, bf16[512,512]{1,0:T(8,128)(2,1)S(1)}, u32[]{:S(2)}, u32[]{:S(2)}) collective-permute-start(bf16[512,512]{1,0:T(8,128)(2,1)S(1)} %get-tuple-element.8), channel_id=1, source_target_pairs={{1,0},{2,1},{3,2},{4,3},{5,4},{6,5},{7,6},{8,7},{9,8},{10,9},{11,1... | collective-permute-start | bytes 1572872 | tf_op jit(solution)/shard_map/ppermute | solution.py:10
  82.5 23.1 %collective-permute-start = (bf16[256,512]{1,0:T(8,128)(2,1)S(1)}, bf16[256,512]{1,0:T(8,128)(2,1)}, u32[]{:S(2)}, u32[]{:S(2)}) collective-permute-start(bf16[256,512]{1,0:T(8,128)(2,1)S(1)} %copy-done.1), channel_id=1, source_target_pairs={{0,2},{1,3},{2,4},{3,5},{4,6},{5,7},{6,8},{7,9},{8,10},{9,11},{10,... | collective-permute-start | bytes 786440 | tf_op jit(solution)/shard_map/ppermute | solution.py:10
  84.5 9.4 %collective-permute-start.6 = (bf16[256,512]{1,0:T(8,128)(2,1)S(1)}, bf16[256,512]{1,0:T(8,128)(2,1)S(1)}, u32[]{:S(2)}, u32[]{:S(2)}) collective-permute-start(bf16[256,512]{1,0:T(8,128)(2,1)S(1)} %copy-done.1), channel_id=1, source_target_pairs={{1,0},{2,1},{3,2},{4,3},{5,4},{6,5},{7,6},{8,7},{9,8},{10,9},{11,1... | collective-permute-start | bytes 786440 | tf_op jit(solution)/shard_map/ppermute | solution.py:10
  88.9 33.1 %collective-permute-start.1 = (bf16[512,512]{1,0:T(8,128)(2,1)}, bf16[512,512]{1,0:T(8,128)(2,1)}, u32[]{:S(2)}, u32[]{:S(2)}) collective-permute-start(bf16[512,512]{1,0:T(8,128)(2,1)} %get-tuple-element.5), channel_id=1, source_target_pairs={{0,2},{1,3},{2,4},{3,5},{4,6},{5,7},{6,8},{7,9},{8,10},{9,11},{10,... | collective-permute-start | bytes 1572872 | tf_op jit(solution)/shard_map/ppermute | solution.py:10
  93.9 28.1 %copy-start.3 = (f32[512]{0:T(512)S(1)}, f32[512]{0:T(512)}, u32[]{:S(2)}) copy-start(f32[512]{0:T(512)} %param.11) | copy-start | bytes 6148
  93.9 28.1 %copy-start.4 = (f32[256]{0:T(256)S(1)}, f32[256]{0:T(256)}, u32[]{:S(2)}) copy-start(f32[256]{0:T(256)} %param.10) | copy-start | bytes 3076
Sparse Core Ops, SparseCore 0:
  10.1 50.2 all-gather.1
where the time goes:
time: 132 us; the launch traced here: 131 us
  waiting for transfers between devices  53.1 us (40%)
  starting transfers between devices  51.3 us (39%)
  between operations  16.8 us (13%)
  matrix products  6.82 us (5%)
  local copies, waits for them, and re-layouts  3.14 us (2%)
    ppermute x12, waiting for transfers between devices, shifted(): return lax.ppermute(block, axis, route)  52.3 us
    ppermute x12, starting transfers between devices, shifted(): return lax.ppermute(block, axis, route)  51.3 us
    dot_general x5, matrix products, block_term(): jnp.dot(left, block, preferred_element_type=jnp.float32)  4.52 us
  transfers between devices with their start and end apart: 13, of which 7 were waited for; matrix products, arithmetic and copies ran while one was open for 6% of the time, Pallas kernels for 0%

commit v1 on v0

v1 whole, which is shorter than its diff:
```python
import jax
import jax.numpy as jnp
from jax import lax
from jax.sharding import PartitionSpec as P


def shifted(block, axis, distance):
    devices = range(lax.axis_size(axis))
    route = [(i - distance, i) for i in devices if i - distance in devices]
    return lax.ppermute(block, axis, route)


def body(amps, integrals, mask, pair_coupling, occ_energy, vir_energy):
    n = lax.axis_size("occ")
    scale = 64.0

    def term(k, left, factor=1.0):
        product = jnp.dot(left, integrals[0, k], preferred_element_type=jnp.float32)
        return product * (mask[0, k].astype(jnp.float32) * factor)

    right2 = term(0, amps, scale).astype(jnp.float16)
    right1 = term(1, amps, scale).astype(jnp.float16)
    far_r2, far_r1 = shifted(right2, "vir", 2), shifted(right1, "vir", 1)
    amps_g, right1_ = lax.optimization_barrier((amps, right1))
    wide = jnp.broadcast_to(amps_g[None], (n, *amps.shape))
    gathered = lax.all_to_all(wide, "occ", 0, 0).reshape(n * amps.shape[0], amps.shape[1])
    amps_l, _ = lax.optimization_barrier((amps_g, wide))
    left2 = term(4, amps_l, scale).astype(jnp.float16)
    left1 = term(3, amps_l, scale).astype(jnp.float16)
    far_l2, far_l1 = shifted(left2, "vir", -2), shifted(left1, "vir", -1)
    own = term(2, amps) + jnp.dot(pair_coupling, gathered, preferred_element_type=jnp.float32)
    far = (far_l2.astype(jnp.float32) + far_l1.astype(jnp.float32)) + (far_r2.astype(jnp.float32) + far_r1.astype(jnp.float32))
    total = own + far * (1.0 / scale)
    return total / (occ_energy[:, None] - vir_energy[None, :])


def solution(mesh):
    placed = (
        P("occ", "vir"),
        P("vir", None, None, None),
        P("vir", None),
        P("occ", None),
        P("occ"),
        P("vir"),
    )
    return jax.shard_map(
        body, mesh=mesh, in_specs=placed, out_specs=P("occ", "vir"), check_vma=False
    )
```

time: 132 us -> 63.8 us (0.48)
  the two profiles are of different devices: /device:TPU:24 before, /device:TPU:58 now
where the time goes in v1:
time: 63.8 us; the launch traced here: 63.2 us
  starting transfers between devices  31.2 us (49%)
  waiting for transfers between devices  12.1 us (19%)
  matrix products  11.3 us (18%)
  local copies, waits for them, and re-layouts  5.44 us (9%)
  between operations  3.17 us (5%)
    ppermute x4, starting transfers between devices, shifted(): return lax.ppermute(block, axis, route)  26.3 us
    ppermute x4, waiting for transfers between devices, shifted(): return lax.ppermute(block, axis, route)  12.1 us
    dot_general x5, matrix products, term(): product = jnp.dot(left, integrals[0, k], preferred_element_type=jnp.float32)  8.3 us
    all_to_all x1, starting transfers between devices, body(): lax.all_to_all(wide, 'occ', 0, 0).reshape(n * amps.shape[0], amps.shape[1])  4.96 us
    dot_general x1, matrix products, body(): jnp.dot(pair_coupling, gathered, preferred_element_type=jnp.float32)  2.96 us
    broadcast_in_dim x1, local copies, waits for them, and re-layouts, body(): wide = jnp.broadcast_to(amps_g[None], (n, *amps.shape))  2.45 us
    slice x1, local copies, waits for them, and re-layouts, term(): return product * (mask[0, k].astype(jnp.float32) * factor)  1.51 us
    unnamed x14, local copies, waits for them, and re-layouts  1.48 us
  transfers between devices with their start and end apart: 5, of which 1 were waited for; matrix products, arithmetic and copies ran while one was open for 10% of the time, Pallas kernels for 0%

profile of v1, /device:TPU:58, one launch (start us, length us, event | category | flops | bytes accessed | tf_op | source)
XLA Modules:
  0.0 63.2 jit_solution(8466088554234016813)
XLA Ops:
  0.0 0.0 copy-start
  0.0 1.5 %fusion.15 = (s32[1,1]{1,0:T(1,128)}, s32[1,1]{1,0:T(1,128)}, s32[1,1]{1,0:T(1,128)}, s32[1,1]{1,0:T(1,128)}, s32[1,1]{1,0:T(1,128)}) fusion(s32[1,5]{1,0:T(1,128)} %param.8), kind=kLoop, calls=%fused_computation.22 | loop fusion | bytes 40 | tf_op jit(solution)/shard_map/slice | solution.py:19
  2.1 2.1 %fusion.1 = f16[256,512]{1,0:T(8,128)(2,1)} fusion(bf16[256,512]{1,0:T(8,128)(2,1)} %param.6, bf16[1,5,512,512]{3,2,1,0:T(8,128)(2,1)} %param.7, f32[]{:T(128)} %bitcast.3), kind=kOutput, calls=%fused_computation.7 | convolution fusion | flops 134479872 | bytes 1049088 | tf_op jit(solution)/shard_map/dot_general | solution.py:18
  4.3 2.5 %broadcast_in_dim.2 = bf16[8,256,512]{2,1,0:T(8,128)(2,1)} broadcast(bf16[256,512]{1,0:T(8,128)(2,1)} %param.6), dimensions={1,2} | broadcast | bytes 2359296 | tf_op jit(solution)/shard_map/broadcast_in_dim | solution.py:25
  6.7 0.0 copy-start.1
  6.7 5.0 %all-to-all-start = ((bf16[8,256,512]{2,1,0:T(8,128)(2,1)}), bf16[8,256,512]{2,1,0:T(8,128)(2,1)S(1)}, u32[]{:S(2)}, u32[]{:S(2)}) async-start(bf16[8,256,512]{2,1,0:T(8,128)(2,1)} %broadcast_in_dim.2), calls=%async_computation | async-start | bytes 4194304 | tf_op jit(solution)/shard_map/all_to_all | solution.py:26
  11.7 0.0 copy-start.5
  11.7 0.0 copy-start.6
  11.7 3.9 %collective-permute-start.3 = (f16[256,512]{1,0:T(8,128)(2,1)}, f16[256,512]{1,0:T(8,128)(2,1)S(1)}, u32[]{:S(2)}, u32[]{:S(2)}) collective-permute-start(f16[256,512]{1,0:T(8,128)(2,1)} %fusion.1), channel_id=1, source_target_pairs={{0,1},{1,2},{2,3},{3,4},{4,5},{5,6},{6,7},{7,8},{8,9},{9,10},{10,1... | collective-permute-start | bytes 786440 | tf_op jit(solution)/shard_map/ppermute | solution.py:10
  16.3 0.0 copy-done.1
  16.3 1.3 %fusion.2 = f16[256,512]{1,0:T(8,128)(2,1)S(1)} fusion(bf16[256,512]{1,0:T(8,128)(2,1)S(1)} %copy-done.1, bf16[1,5,512,512]{3,2,1,0:T(8,128)(2,1)} %param.7, f32[]{:T(128)} %bitcast.7), kind=kOutput, calls=%fused_computation.8 | convolution fusion | flops 134479872 | bytes 1049088 | tf_op jit(solution)/shard_map/dot_general | solution.py:18
  17.6 16.5 %collective-permute-start = (f16[256,512]{1,0:T(8,128)(2,1)S(1)}, f16[256,512]{1,0:T(8,128)(2,1)S(1)}, u32[]{:S(2)}, u32[]{:S(2)}) collective-permute-start(f16[256,512]{1,0:T(8,128)(2,1)S(1)} %fusion.2), channel_id=1, source_target_pairs={{2,0},{3,1},{4,2},{5,3},{6,4},{7,5},{8,6},{9,7},{10,8},{11,9},{12,... | collective-permute-start | bytes 786440 | tf_op jit(solution)/shard_map/ppermute | solution.py:10
  34.8 1.3 %fusion.3 = f16[256,512]{1,0:T(8,128)(2,1)S(1)} fusion(bf16[256,512]{1,0:T(8,128)(2,1)S(1)} %copy-done.1, bf16[1,5,512,512]{3,2,1,0:T(8,128)(2,1)} %param.7, f32[]{:T(128)} %bitcast.9), kind=kOutput, calls=%fused_computation.9 | convolution fusion | flops 134479872 | bytes 1049088 | tf_op jit(solution)/shard_map/dot_general | solution.py:18
  36.2 3.9 %collective-permute-start.1 = (f16[256,512]{1,0:T(8,128)(2,1)S(1)}, f16[256,512]{1,0:T(8,128)(2,1)S(1)}, u32[]{:S(2)}, u32[]{:S(2)}) collective-permute-start(f16[256,512]{1,0:T(8,128)(2,1)S(1)} %fusion.3), channel_id=1, source_target_pairs={{1,0},{2,1},{3,2},{4,3},{5,4},{6,5},{7,6},{8,7},{9,8},{10,9},{11,1... | collective-permute-start | bytes 786440 | tf_op jit(solution)/shard_map/ppermute | solution.py:10
  40.7 1.3 %fusion.4 = f16[256,512]{1,0:T(8,128)(2,1)S(1)} fusion(bf16[256,512]{1,0:T(8,128)(2,1)S(1)} %copy-done.1, bf16[1,5,512,512]{3,2,1,0:T(8,128)(2,1)} %param.7, f32[]{:T(128)} %bitcast.11), kind=kOutput, calls=%fused_computation.10 | convolution fusion | flops 134479872 | bytes 1049088 | tf_op jit(solution)/shard_map/dot_general | solution.py:18
  42.0 1.9 %collective-permute-start.2 = (f16[256,512]{1,0:T(8,128)(2,1)S(1)}, f16[256,512]{1,0:T(8,128)(2,1)}, u32[]{:S(2)}, u32[]{:S(2)}) collective-permute-start(f16[256,512]{1,0:T(8,128)(2,1)S(1)} %fusion.4), channel_id=1, source_target_pairs={{0,2},{1,3},{2,4},{3,5},{4,6},{5,7},{6,8},{7,9},{8,10},{9,11},{10,... | collective-permute-start | bytes 786440 | tf_op jit(solution)/shard_map/ppermute | solution.py:10
  44.5 2.1 %convolution_multiply_fusion.4 = f32[256,512]{1,0:T(8,128)} fusion(bf16[256,512]{1,0:T(8,128)(2,1)S(1)} %copy-done.1, bf16[1,5,512,512]{3,2,1,0:T(8,128)(2,1)} %param.7, f32[]{:T(128)} %bitcast.1), kind=kOutput, calls=%fused_computation.6 | convolution fusion | flops 134348800 | bytes 1311232 | tf_op jit(solution)/shard_map/dot_general | solution.py:18
  46.7 0.0 collective-permute-done
  46.7 0.0 copy-start.3
  46.7 0.0 collective-permute-done.1
  46.7 0.0 copy-start.4
  46.7 0.0 collective-permute-done.3
  46.7 0.7 %copy-done.3 = f16[256,512]{1,0:T(8,128)(2,1)} copy-done((f16[256,512]{1,0:T(8,128)(2,1)}, f16[256,512]{1,0:T(8,128)(2,1)S(1)}, u32[]{:S(2)}) %copy-start.3) | copy-done | bytes 262168
  47.4 0.1 copy-done.4
  47.4 0.0 copy-start.2
  47.4 0.7 %copy-done.2 = f16[256,512]{1,0:T(8,128)(2,1)} copy-done((f16[256,512]{1,0:T(8,128)(2,1)}, f16[256,512]{1,0:T(8,128)(2,1)S(1)}, u32[]{:S(2)}) %copy-start.2) | copy-done | bytes 262168
  48.1 12.0 %collective-permute-done.2 = f16[256,512]{1,0:T(8,128)(2,1)} collective-permute-done((f16[256,512]{1,0:T(8,128)(2,1)S(1)}, f16[256,512]{1,0:T(8,128)(2,1)}, u32[]{:S(2)}, u32[]{:S(2)}) %collective-permute-start.2) | collective-permute-done | bytes 262176 | tf_op jit(solution)/shard_map/ppermute | solution.py:10
  60.2 0.0 all-to-all-done
  60.2 0.0 copy-done
  60.2 0.0 copy-done.5
  60.2 0.0 copy-done.6
  60.2 3.0 %subtract_divide_fusion = f32[256,512]{1,0:T(8,128)} fusion(f16[256,512]{1,0:T(8,128)(2,1)} %copy-done.2, f16[256,512]{1,0:T(8,128)(2,1)} %collective-permute-done.2, f16[256,512]{1,0:T(8,128)(2,1)} %copy-done.4, f16[256,512]{1,0:T(8,128)(2,1)} %copy-done.3, f32[512]{0:T(512)S(1)} %copy-done.5, f32[256]{0:T(256)S(1)} %copy-done.6, ...), kind=kOutput, calls=%fused_computation.16 | convolution fusion | flops 538443776 | bytes 5245952 | tf_op jit(solution)/shard_map/dot_general | solution.py:31
Async XLA Ops:
  0.0 60.2 %copy-start = (bf16[256,2048]{1,0:T(8,128)(2,1)S(1)}, bf16[256,2048]{1,0:T(8,128)(2,1)}, u32[]{:S(2)}) copy-start(bf16[256,2048]{1,0:T(8,128)(2,1)} %param.9) | copy-start | bytes 3145732
  6.7 9.6 %copy-start.1 = (bf16[256,512]{1,0:T(8,128)(2,1)S(1)}, bf16[256,512]{1,0:T(8,128)(2,1)}, u32[]{:S(2)}) copy-start(bf16[256,512]{1,0:T(8,128)(2,1)} %param.6) | copy-start | bytes 786436
  6.7 53.5 %all-to-all-start = ((bf16[8,256,512]{2,1,0:T(8,128)(2,1)}), bf16[8,256,512]{2,1,0:T(8,128)(2,1)S(1)}, u32[]{:S(2)}, u32[]{:S(2)}) async-start(bf16[8,256,512]{2,1,0:T(8,128)(2,1)} %broadcast_in_dim.2), calls=%async_computation | async-start | bytes 4194304 | tf_op jit(solution)/shard_map/all_to_all | solution.py:26
  11.7 48.5 %copy-start.5 = (f32[512]{0:T(512)S(1)}, f32[512]{0:T(512)}, u32[]{:S(2)}) copy-start(f32[512]{0:T(512)} %param.11) | copy-start | bytes 6148
  11.7 48.5 %copy-start.6 = (f32[256]{0:T(256)S(1)}, f32[256]{0:T(256)}, u32[]{:S(2)}) copy-start(f32[256]{0:T(256)} %param.10) | copy-start | bytes 3076
  11.7 35.0 %collective-permute-start.3 = (f16[256,512]{1,0:T(8,128)(2,1)}, f16[256,512]{1,0:T(8,128)(2,1)S(1)}, u32[]{:S(2)}, u32[]{:S(2)}) collective-permute-start(f16[256,512]{1,0:T(8,128)(2,1)} %fusion.1), channel_id=1, source_target_pairs={{0,1},{1,2},{2,3},{3,4},{4,5},{5,6},{6,7},{7,8},{8,9},{9,10},{10,1... | collective-permute-start | bytes 786440 | tf_op jit(solution)/shard_map/ppermute | solution.py:10
  17.6 29.0 %collective-permute-start = (f16[256,512]{1,0:T(8,128)(2,1)S(1)}, f16[256,512]{1,0:T(8,128)(2,1)S(1)}, u32[]{:S(2)}, u32[]{:S(2)}) collective-permute-start(f16[256,512]{1,0:T(8,128)(2,1)S(1)} %fusion.2), channel_id=1, source_target_pairs={{2,0},{3,1},{4,2},{5,3},{6,4},{7,5},{8,6},{9,7},{10,8},{11,9},{12,... | collective-permute-start | bytes 786440 | tf_op jit(solution)/shard_map/ppermute | solution.py:10
  36.2 10.5 %collective-permute-start.1 = (f16[256,512]{1,0:T(8,128)(2,1)S(1)}, f16[256,512]{1,0:T(8,128)(2,1)S(1)}, u32[]{:S(2)}, u32[]{:S(2)}) collective-permute-start(f16[256,512]{1,0:T(8,128)(2,1)S(1)} %fusion.3), channel_id=1, source_target_pairs={{1,0},{2,1},{3,2},{4,3},{5,4},{6,5},{7,6},{8,7},{9,8},{10,9},{11,1... | collective-permute-start | bytes 786440 | tf_op jit(solution)/shard_map/ppermute | solution.py:10
  42.0 18.1 %collective-permute-start.2 = (f16[256,512]{1,0:T(8,128)(2,1)S(1)}, f16[256,512]{1,0:T(8,128)(2,1)}, u32[]{:S(2)}, u32[]{:S(2)}) collective-permute-start(f16[256,512]{1,0:T(8,128)(2,1)S(1)} %fusion.4), channel_id=1, source_target_pairs={{0,2},{1,3},{2,4},{3,5},{4,6},{5,7},{6,8},{7,9},{8,10},{9,11},{10,... | collective-permute-start | bytes 786440 | tf_op jit(solution)/shard_map/ppermute | solution.py:10
  46.7 0.7 %copy-start.3 = (f16[256,512]{1,0:T(8,128)(2,1)}, f16[256,512]{1,0:T(8,128)(2,1)S(1)}, u32[]{:S(2)}) copy-start(f16[256,512]{1,0:T(8,128)(2,1)S(1)} %collective-permute-done) | copy-start | bytes 786436
  46.7 0.8 %copy-start.4 = (f16[256,512]{1,0:T(8,128)(2,1)}, f16[256,512]{1,0:T(8,128)(2,1)S(1)}, u32[]{:S(2)}) copy-start(f16[256,512]{1,0:T(8,128)(2,1)S(1)} %collective-permute-done.1) | copy-start | bytes 786436
  47.4 0.7 %copy-start.2 = (f16[256,512]{1,0:T(8,128)(2,1)}, f16[256,512]{1,0:T(8,128)(2,1)S(1)}, u32[]{:S(2)}) copy-start(f16[256,512]{1,0:T(8,128)(2,1)S(1)} %collective-permute-done.3) | copy-start | bytes 786436

commit v2 on v1

v2 whole, which is shorter than its diff:
```python
import jax
import jax.numpy as jnp
from jax import lax
from jax.experimental import pallas as pl
from jax.experimental.pallas import tpu as pltpu
from jax.sharding import PartitionSpec as P

SCALE = 64.0
SENT = (1, 0, 3, 4)
CORES = 2
STEPS = (0, 2, 6, 4)
LIMIT = 8 * 2**20


def shifted(block, axis, distance):
    devices = range(lax.axis_size(axis))
    route = [(i - distance, i) for i in devices if i - distance in devices]
    return lax.ppermute(block, axis, route)


def terms_kernel(mask_ref, amps_ref, blocks_ref, *rest):
    out_refs, (held, sems) = rest[:4], rest[4:]
    loads = [
        pltpu.make_async_copy(blocks_ref.at[0, k], held.at[i], sems.at[i])
        for i, k in enumerate(SENT)
    ]
    for load in loads:
        load.start()
    for i, k in enumerate(SENT):
        loads[i].wait()
        flag = mask_ref[0, k].astype(jnp.float32) * SCALE
        out_refs[i][...] = flag * jnp.dot(
            amps_ref[...], held[i], preferred_element_type=jnp.float32
        )


def terms(mask, amps, integrals):
    rows, tile = amps.shape
    whole = pl.BlockSpec(memory_space=pltpu.VMEM)
    return pl.pallas_call(
        terms_kernel,
        out_shape=(jax.ShapeDtypeStruct((rows, tile), jnp.float32),) * 4,
        in_specs=[pl.BlockSpec(memory_space=pltpu.SMEM), whole, pl.BlockSpec(memory_space=pl.ANY)],
        out_specs=(whole,) * 4,
        scratch_shapes=[pltpu.VMEM((4, tile, tile), amps.dtype), pltpu.SemaphoreType.DMA((4,))],
        compiler_params=pltpu.CompilerParams(vmem_limit_bytes=LIMIT),
        cost_estimate=pl.CostEstimate(
            flops=8 * rows * tile * tile, bytes_accessed=8 * tile * tile, transcendentals=0
        ),
    )(mask, amps, integrals)


def join_kernel(*refs):
    for i, ref in enumerate(refs[:-1]):
        refs[-1][i] = ref[...]


def joined(parts):
    whole = pl.BlockSpec(memory_space=pltpu.VMEM)
    return pl.pallas_call(
        join_kernel,
        out_shape=jax.ShapeDtypeStruct((len(parts), *parts[0].shape), parts[0].dtype),
        in_specs=[whole] * len(parts),
        out_specs=whole,
        compiler_params=pltpu.CompilerParams(vmem_limit_bytes=LIMIT),
        cost_estimate=pl.CostEstimate(flops=0, bytes_accessed=4 * len(parts) * parts[0].size, transcendentals=0),
    )(*parts)


def columns_of(coupling_ref, place, core, rows):
    devices = lax.axis_size("occ")
    me = lax.axis_index("occ")
    me = me - lax.rem(me, CORES) + core
    start = pl.multiple_of(lax.rem(me - STEPS[place] + devices, devices) * rows, rows)
    return coupling_ref[:, pl.ds(start, rows)]


def near_kernel(mask_ref, amps_ref, blocks_ref, coupling_ref, near_ref, total_ref, held, sem):
    load = pltpu.make_async_copy(blocks_ref.at[0, 2], held, sem)
    load.start()
    core = lax.rem(lax.axis_index("occ"), CORES)
    chips, rows = near_ref.shape[:2]
    total = jnp.zeros(total_ref.shape, jnp.float32)
    for chip in range(chips):
        total += jnp.dot(
            columns_of(coupling_ref, chip, core, rows), near_ref[chip], preferred_element_type=jnp.float32
        )
    load.wait()
    flag = mask_ref[0, 2].astype(jnp.float32)
    total_ref[...] = total + flag * jnp.dot(amps_ref[...], held[...], preferred_element_type=jnp.float32)


def near_terms(mask, amps, integrals, coupling, near):
    rows, tile = amps.shape
    whole = pl.BlockSpec(memory_space=pltpu.VMEM)
    return pl.pallas_call(
        near_kernel,
        out_shape=jax.ShapeDtypeStruct((rows, tile), jnp.float32),
        in_specs=[pl.BlockSpec(memory_space=pltpu.SMEM), whole, pl.BlockSpec(memory_space=pl.ANY), whole, whole],
        out_specs=whole,
        scratch_shapes=[pltpu.VMEM((tile, tile), amps.dtype), pltpu.SemaphoreType.DMA],
        compiler_params=pltpu.CompilerParams(vmem_limit_bytes=LIMIT),
        cost_estimate=pl.CostEstimate(
            flops=16 * coupling.size * tile, bytes_accessed=2 * (coupling.size + near.size), transcendentals=0
        ),
    )(mask, amps, integrals, coupling, near)


def far_kernel(coupling_ref, far_ref, total_ref, sum_ref):
    core = CORES - 1 - lax.rem(lax.axis_index("occ"), CORES)
    chips, rows = far_ref.shape[:2]
    total = total_ref[...]
    for chip in range(chips):
        total += jnp.dot(
            columns_of(coupling_ref, chip, core, rows), far_ref[chip], preferred_element_type=jnp.float32
        )
    sum_ref[...] = total


def far_terms(coupling, far, total):
    whole = pl.BlockSpec(memory_space=pltpu.VMEM)
    return pl.pallas_call(
        far_kernel,
        out_shape=jax.ShapeDtypeStruct(total.shape, jnp.float32),
        in_specs=[whole] * 3,
        out_specs=whole,
        compiler_params=pltpu.CompilerParams(vmem_limit_bytes=LIMIT),
        cost_estimate=pl.CostEstimate(
            flops=coupling.size * total.shape[1], bytes_accessed=2 * (coupling.size + far.size), transcendentals=0
        ),
    )(coupling, far, total)


def body(amps, integrals, mask, pair_coupling, occ_energy, vir_energy):
    devices = lax.axis_size("occ")
    rows = [amps] + [
        lax.ppermute(amps, "occ", [(i, (i + step) % devices) for i in range(devices)]) for step in STEPS[1:]
    ]
    products = terms(mask, amps, integrals)
    arrived = [
        shifted(products[i].astype(jnp.float16), "vir", (1, 2, -1, -2)[i]) for i in (3, 2, 1, 0)
    ]
    near = joined(rows)
    far = lax.ppermute(near, "occ", [(i, i ^ 1) for i in range(devices)])
    total = near_terms(mask, amps, integrals, pair_coupling, near)
    total = far_terms(pair_coupling, far, total)
    total = total + sum(a.astype(jnp.float32) for a in arrived) * (1.0 / SCALE)
    return total / (occ_energy[:, None] - vir_energy[None, :])


def solution(mesh):
    placed = (
        P("occ", "vir"),
        P("vir", None, None, None),
        P("vir", None),
        P("occ", None),
        P("occ"),
        P("vir"),
    )
    return jax.shard_map(
        body, mesh=mesh, in_specs=placed, out_specs=P("occ", "vir"), check_vma=False
    )
```

time: 63.8 us -> 67.8 us (1.063)
  the two profiles are of different devices: /device:TPU:58 before, /device:TPU:24 now
where the time goes in v2:
time: 67.8 us; the launch traced here: 67.5 us
  starting transfers between devices  40.2 us (59%)
  waiting for transfers between devices  18.7 us (28%)
  Pallas kernels  3.77 us (6%)
  local copies, waits for them, and re-layouts  3.37 us (5%)
  other arithmetic  1.18 us (2%)
    ppermute x4, starting transfers between devices, shifted(): return lax.ppermute(block, axis, route)  27.5 us
    ppermute x3, starting transfers between devices, body(): lax.ppermute(amps, 'occ', [(i, (i + step) % devices) for i in range(devic...  10.8 us
    ppermute x4, waiting for transfers between devices, shifted(): return lax.ppermute(block, axis, route)  10.7 us
    ppermute x3, waiting for transfers between devices, body(): lax.ppermute(amps, 'occ', [(i, (i + step) % devices) for i in range(devic...  8 us
    unnamed x18, local copies, waits for them, and re-layouts  3.37 us
    pallas_call x1, Pallas kernels, terms(): pl.pallas_call(terms_kernel, out_shape=(jax.ShapeDtypeStruct((rows, tile)...  1.94 us
    ppermute x1, starting transfers between devices, body(): far = lax.ppermute(near, 'occ', [(i, i ^ 1) for i in range(devices)])  1.92 us
  transfers between devices with their start and end apart: 8, of which 5 were waited for; matrix products, arithmetic and copies ran while one was open for 0% of the time, Pallas kernels for 5%

profile of v2, /device:TPU:24, one launch (start us, length us, event | category | flops | bytes accessed | tf_op | source)
XLA Modules:
  0.0 67.5 jit_solution(8550595334330815319)
XLA Ops:
  0.0 4.9 %collective-permute-start.2 = (bf16[256,512]{1,0:T(8,128)(2,1)}, bf16[256,512]{1,0:T(8,128)(2,1)S(1)}, u32[]{:S(2)}, u32[]{:S(2)}) collective-permute-start(bf16[256,512]{1,0:T(8,128)(2,1)} %amps_ref.3), channel_id=1, source_target_pairs={{0,512},{128,640},{256,768},{384,896},{512,0},{640,128},{768,256},... | collective-permute-start | bytes 786440 | tf_op jit(solution)/shard_map/ppermute | solution.py:137
  4.9 3.1 %collective-permute-start.1 = (bf16[256,512]{1,0:T(8,128)(2,1)}, bf16[256,512]{1,0:T(8,128)(2,1)S(1)}, u32[]{:S(2)}, u32[]{:S(2)}) collective-permute-start(bf16[256,512]{1,0:T(8,128)(2,1)} %amps_ref.3), channel_id=1, source_target_pairs={{0,768},{128,896},{256,0},{384,128},{512,256},{640,384},{768,512},... | collective-permute-start | bytes 786440 | tf_op jit(solution)/shard_map/ppermute | solution.py:137
  8.0 2.8 %collective-permute-start = (bf16[256,512]{1,0:T(8,128)(2,1)}, bf16[256,512]{1,0:T(8,128)(2,1)S(1)}, u32[]{:S(2)}, u32[]{:S(2)}) collective-permute-start(bf16[256,512]{1,0:T(8,128)(2,1)} %amps_ref.3), channel_id=1, source_target_pairs={{0,256},{128,384},{256,512},{384,640},{512,768},{640,896},{768,0},... | collective-permute-start | bytes 786440 | tf_op jit(solution)/shard_map/ppermute | solution.py:137
  10.8 0.9 %collective-permute-done.2.refs_3_ = bf16[256,512]{1,0:T(8,128)(2,1)S(1)} collective-permute-done((bf16[256,512]{1,0:T(8,128)(2,1)}, bf16[256,512]{1,0:T(8,128)(2,1)S(1)}, u32[]{:S(2)}, u32[]{:S(2)}) %collective-permute-start.2) | collective-permute-done | bytes 262176 | tf_op jit(solution)/shard_map/ppermute | solution.py:137
  11.6 5.7 %collective-permute-done.1.refs_2_ = bf16[256,512]{1,0:T(8,128)(2,1)S(1)} collective-permute-done((bf16[256,512]{1,0:T(8,128)(2,1)}, bf16[256,512]{1,0:T(8,128)(2,1)S(1)}, u32[]{:S(2)}, u32[]{:S(2)}) %collective-permute-start.1) | collective-permute-done | bytes 262176 | tf_op jit(solution)/shard_map/ppermute | solution.py:137
  17.4 1.4 %collective-permute-done.refs_1_ = bf16[256,512]{1,0:T(8,128)(2,1)S(1)} collective-permute-done((bf16[256,512]{1,0:T(8,128)(2,1)}, bf16[256,512]{1,0:T(8,128)(2,1)S(1)}, u32[]{:S(2)}, u32[]{:S(2)}) %collective-permute-start) | collective-permute-done | bytes 262176 | tf_op jit(solution)/shard_map/ppermute | solution.py:137
  18.8 0.9 %copy-done.3 = bf16[256,512]{1,0:T(8,128)(2,1)S(1)} copy-done((bf16[256,512]{1,0:T(8,128)(2,1)S(1)}, bf16[256,512]{1,0:T(8,128)(2,1)}, u32[]{:S(2)}) %copy-start.3) | copy-done | bytes 262168
  19.7 0.1 shard_map.64.near_ref
  19.8 1.9 %collective-permute-start.3 = (bf16[4,256,512]{2,1,0:T(8,128)(2,1)S(1)}, bf16[4,256,512]{2,1,0:T(8,128)(2,1)S(1)}, u32[]{:S(2)}, u32[]{:S(2)}) collective-permute-start(bf16[4,256,512]{2,1,0:T(8,128)(2,1)S(1)} %shard_map.64.near_ref), channel_id=1, source_target_pairs={{0,128},{128,0},{256,384},{384,256},{512,640},{640,512},{768,896},... | collective-permute-start | bytes 3145736 | tf_op jit(solution)/shard_map/ppermute | solution.py:144
  21.7 0.0 copy-start
  21.8 1.7 %copy-done = bf16[1,5,512,512]{3,2,1,0:T(8,128)(2,1)S(1)} copy-done((bf16[1,5,512,512]{3,2,1,0:T(8,128)(2,1)S(1)}, bf16[1,5,512,512]{3,2,1,0:T(8,128)(2,1)}, u32[]{:S(2)}) %copy-start) | copy-done | bytes 2621464
  23.5 0.7 copy-done.5
  24.2 1.9 %shard_map.67 = (f32[256,512]{1,0:T(8,128)S(1)}, f32[256,512]{1,0:T(8,128)S(1)}, f32[256,512]{1,0:T(8,128)S(1)}, f32[256,512]{1,0:T(8,128)S(1)}) custom-call(s32[1,5]{1,0:T(1,128)S(1)} %copy-done.5, bf16[256,512]{1,0:T(8,128)(2,1)S(1)} %copy-done.3, bf16[1,5,512,512]{3,2,1,0:T(8,128)(2,1)S(1)} %copy-done), custom_call_target="tpu_custom_call" | custom-call | flops 536870912 | bytes 2097152 | tf_op jit(solution)/shard_map/pallas_call | solution.py:40
  26.1 3.8 %collective-permute-start.7 = (f16[256,512]{1,0:T(8,128)(2,1)S(1)}, f16[256,512]{1,0:T(8,128)(2,1)S(1)}, u32[]{:S(2)}, u32[]{:S(2)}) collective-permute-start(f16[256,512]{1,0:T(8,128)(2,1)S(1)} %convert_element_type.30), channel_id=1, source_target_pairs={{0,1},{1,2},{2,3},{3,4},{4,5},{5,6},{6,7},{7,8},{8,9},{9,10},{10,1... | collective-permute-start | bytes 786440 | tf_op jit(solution)/shard_map/ppermute | solution.py:18
  30.0 5.2 %collective-permute-start.6 = (f16[256,512]{1,0:T(8,128)(2,1)S(1)}, f16[256,512]{1,0:T(8,128)(2,1)S(1)}, u32[]{:S(2)}, u32[]{:S(2)}) collective-permute-start(f16[256,512]{1,0:T(8,128)(2,1)S(1)} %convert_element_type.28), channel_id=1, source_target_pairs={{0,2},{1,3},{2,4},{3,5},{4,6},{5,7},{6,8},{7,9},{8,10},{9,11},{10,... | collective-permute-start | bytes 786440 | tf_op jit(solution)/shard_map/ppermute | solution.py:18
  35.3 13.7 %collective-permute-start.5 = (f16[256,512]{1,0:T(8,128)(2,1)S(1)}, f16[256,512]{1,0:T(8,128)(2,1)S(1)}, u32[]{:S(2)}, u32[]{:S(2)}) collective-permute-start(f16[256,512]{1,0:T(8,128)(2,1)S(1)} %convert_element_type.26), channel_id=1, source_target_pairs={{1,0},{2,1},{3,2},{4,3},{5,4},{6,5},{7,6},{8,7},{9,8},{10,9},{11,1... | collective-permute-start | bytes 786440 | tf_op jit(solution)/shard_map/ppermute | solution.py:18
  49.0 4.8 %collective-permute-start.4 = (f16[256,512]{1,0:T(8,128)(2,1)S(1)}, f16[256,512]{1,0:T(8,128)(2,1)S(1)}, u32[]{:S(2)}, u32[]{:S(2)}) collective-permute-start(f16[256,512]{1,0:T(8,128)(2,1)S(1)} %convert_element_type.24), channel_id=1, source_target_pairs={{2,0},{3,1},{4,2},{5,3},{6,4},{7,5},{8,6},{9,7},{10,8},{11,9},{12,... | collective-permute-start | bytes 786440 | tf_op jit(solution)/shard_map/ppermute | solution.py:18
  53.8 0.0 copy-done.1
  53.8 0.0 copy-done.2
  53.9 0.0 copy-done.4
  53.9 0.0 copy-done.6
  53.9 1.3 %shard_map.65.total_ref = f32[256,512]{1,0:T(8,128)S(1)} custom-call(s32[1,5]{1,0:T(1,128)S(1)} %copy-done.6, bf16[256,512]{1,0:T(8,128)(2,1)S(1)} %copy-done.4, bf16[1,5,512,512]{3,2,1,0:T(8,128)(2,1)S(1)} %copy-done.1, bf16[256,2048]{1,0:T(8,128)(2,1)S(1)} %copy-done.2, bf16[4,256,512]{2,1,0:T(8,128)(2,1)S(1)} %shard_map.64.near_ref), custom_call_target="tpu_custom_call" | custom-call | flops 4294967296 | bytes 2097152 | tf_op jit(solution)/shard_map/pallas_call | solution.py:96
  55.2 0.0 copy-start.7
  55.2 0.0 copy-start.8
  55.2 0.0 collective-permute-done.3.far_ref
  55.2 0.4 shard_map.66
  55.7 0.0 collective-permute-done.7
  55.7 5.4 %collective-permute-done.6 = f16[256,512]{1,0:T(8,128)(2,1)S(1)} collective-permute-done((f16[256,512]{1,0:T(8,128)(2,1)S(1)}, f16[256,512]{1,0:T(8,128)(2,1)S(1)}, u32[]{:S(2)}, u32[]{:S(2)}) %collective-permute-start.6) | collective-permute-done | bytes 262176 | tf_op jit(solution)/shard_map/ppermute | solution.py:18
  61.1 0.0 collective-permute-done.5
  61.1 5.4 %collective-permute-done.4 = f16[256,512]{1,0:T(8,128)(2,1)S(1)} collective-permute-done((f16[256,512]{1,0:T(8,128)(2,1)S(1)}, f16[256,512]{1,0:T(8,128)(2,1)S(1)}, u32[]{:S(2)}, u32[]{:S(2)}) %collective-permute-start.4) | collective-permute-done | bytes 262176 | tf_op jit(solution)/shard_map/ppermute | solution.py:18
  66.4 0.0 copy-done.7
  66.5 1.0 %subtract_divide_fusion = f32[256,512]{1,0:T(8,128)} fusion(f32[256,512]{1,0:T(8,128)S(1)} %shard_map.66, f16[256,512]{1,0:T(8,128)(2,1)S(1)} %collective-permute-done.7, f16[256,512]{1,0:T(8,128)(2,1)S(1)} %collective-permute-done.6, f16[256,512]{1,0:T(8,128)(2,1)S(1)} %collective-permute-done.5, f16[256,512]{1,0:T(8,128)(2,1)S(1)} %collective-permute-done.4, ...), kind=kLoop, calls=%fused_computation | loop fusion | flops 1441792 | bytes 2100224 | tf_op jit(solution)/shard_map/div | solution.py:148
  (11 shorter events, 0.2 us)
Async XLA Ops:
  0.0 11.6 %collective-permute-start.2 = (bf16[256,512]{1,0:T(8,128)(2,1)}, bf16[256,512]{1,0:T(8,128)(2,1)S(1)}, u32[]{:S(2)}, u32[]{:S(2)}) collective-permute-start(bf16[256,512]{1,0:T(8,128)(2,1)} %amps_ref.3), channel_id=1, source_target_pairs={{0,512},{128,640},{256,768},{384,896},{512,0},{640,128},{768,256},... | collective-permute-start | bytes 786440 | tf_op jit(solution)/shard_map/ppermute | solution.py:137
  4.9 12.4 %collective-permute-start.1 = (bf16[256,512]{1,0:T(8,128)(2,1)}, bf16[256,512]{1,0:T(8,128)(2,1)S(1)}, u32[]{:S(2)}, u32[]{:S(2)}) collective-permute-start(bf16[256,512]{1,0:T(8,128)(2,1)} %amps_ref.3), channel_id=1, source_target_pairs={{0,768},{128,896},{256,0},{384,128},{512,256},{640,384},{768,512},... | collective-permute-start | bytes 786440 | tf_op jit(solution)/shard_map/ppermute | solution.py:137
  8.0 10.8 %collective-permute-start = (bf16[256,512]{1,0:T(8,128)(2,1)}, bf16[256,512]{1,0:T(8,128)(2,1)S(1)}, u32[]{:S(2)}, u32[]{:S(2)}) collective-permute-start(bf16[256,512]{1,0:T(8,128)(2,1)} %amps_ref.3), channel_id=1, source_target_pairs={{0,256},{128,384},{256,512},{384,640},{512,768},{640,896},{768,0},... | collective-permute-start | bytes 786440 | tf_op jit(solution)/shard_map/ppermute | solution.py:137
  18.8 1.0 %copy-start.3 = (bf16[256,512]{1,0:T(8,128)(2,1)S(1)}, bf16[256,512]{1,0:T(8,128)(2,1)}, u32[]{:S(2)}) copy-start(bf16[256,512]{1,0:T(8,128)(2,1)} %amps_ref.3) | copy-start | bytes 786436
  19.8 35.4 %collective-permute-start.3 = (bf16[4,256,512]{2,1,0:T(8,128)(2,1)S(1)}, bf16[4,256,512]{2,1,0:T(8,128)(2,1)S(1)}, u32[]{:S(2)}, u32[]{:S(2)}) collective-permute-start(bf16[4,256,512]{2,1,0:T(8,128)(2,1)S(1)} %shard_map.64.near_ref), channel_id=1, source_target_pairs={{0,128},{128,0},{256,384},{384,256},{512,640},{640,512},{768,896},... | collective-permute-start | bytes 3145736 | tf_op jit(solution)/shard_map/ppermute | solution.py:144
  21.7 1.7 %copy-start = (bf16[1,5,512,512]{3,2,1,0:T(8,128)(2,1)S(1)}, bf16[1,5,512,512]{3,2,1,0:T(8,128)(2,1)}, u32[]{:S(2)}) copy-start(bf16[1,5,512,512]{3,2,1,0:T(8,128)(2,1)} %blocks_ref.3) | copy-start | bytes 7864324
  23.5 0.7 copy-start.5
  24.1 29.7 %copy-start.1 = (bf16[1,5,512,512]{3,2,1,0:T(8,128)(2,1)S(1)}, bf16[1,5,512,512]{3,2,1,0:T(8,128)(2,1)}, u32[]{:S(2)}) copy-start(bf16[1,5,512,512]{3,2,1,0:T(8,128)(2,1)} %blocks_ref.3) | copy-start | bytes 7864324
  24.1 29.7 %copy-start.2 = (bf16[256,2048]{1,0:T(8,128)(2,1)S(1)}, bf16[256,2048]{1,0:T(8,128)(2,1)}, u32[]{:S(2)}) copy-start(bf16[256,2048]{1,0:T(8,128)(2,1)} %coupling_ref.3) | copy-start | bytes 3145732
  24.1 29.7 %copy-start.4 = (bf16[256,512]{1,0:T(8,128)(2,1)S(1)}, bf16[256,512]{1,0:T(8,128)(2,1)}, u32[]{:S(2)}) copy-start(bf16[256,512]{1,0:T(8,128)(2,1)} %amps_ref.3) | copy-start | bytes 786436
  24.1 29.7 %copy-start.6 = (s32[1,5]{1,0:T(1,128)S(1)}, s32[1,5]{1,0:T(1,128)}, u32[]{:S(2)}) copy-start(s32[1,5]{1,0:T(1,128)} %mask_ref.3) | copy-start | bytes 64
  26.1 29.5 %collective-permute-start.7 = (f16[256,512]{1,0:T(8,128)(2,1)S(1)}, f16[256,512]{1,0:T(8,128)(2,1)S(1)}, u32[]{:S(2)}, u32[]{:S(2)}) collective-permute-start(f16[256,512]{1,0:T(8,128)(2,1)S(1)} %convert_element_type.30), channel_id=1, source_target_pairs={{0,1},{1,2},{2,3},{3,4},{4,5},{5,6},{6,7},{7,8},{8,9},{9,10},{10,1... | collective-permute-start | bytes 786440 | tf_op jit(solution)/shard_map/ppermute | solution.py:18
  30.0 31.1 %collective-permute-start.6 = (f16[256,512]{1,0:T(8,128)(2,1)S(1)}, f16[256,512]{1,0:T(8,128)(2,1)S(1)}, u32[]{:S(2)}, u32[]{:S(2)}) collective-permute-start(f16[256,512]{1,0:T(8,128)(2,1)S(1)} %convert_element_type.28), channel_id=1, source_target_pairs={{0,2},{1,3},{2,4},{3,5},{4,6},{5,7},{6,8},{7,9},{8,10},{9,11},{10,... | collective-permute-start | bytes 786440 | tf_op jit(solution)/shard_map/ppermute | solution.py:18
  35.3 25.8 %collective-permute-start.5 = (f16[256,512]{1,0:T(8,128)(2,1)S(1)}, f16[256,512]{1,0:T(8,128)(2,1)S(1)}, u32[]{:S(2)}, u32[]{:S(2)}) collective-permute-start(f16[256,512]{1,0:T(8,128)(2,1)S(1)} %convert_element_type.26), channel_id=1, source_target_pairs={{1,0},{2,1},{3,2},{4,3},{5,4},{6,5},{7,6},{8,7},{9,8},{10,9},{11,1... | collective-permute-start | bytes 786440 | tf_op jit(solution)/shard_map/ppermute | solution.py:18
  49.0 17.4 %collective-permute-start.4 = (f16[256,512]{1,0:T(8,128)(2,1)S(1)}, f16[256,512]{1,0:T(8,128)(2,1)S(1)}, u32[]{:S(2)}, u32[]{:S(2)}) collective-permute-start(f16[256,512]{1,0:T(8,128)(2,1)S(1)} %convert_element_type.24), channel_id=1, source_target_pairs={{2,0},{3,1},{4,2},{5,3},{6,4},{7,5},{8,6},{9,7},{10,8},{11,9},{12,... | collective-permute-start | bytes 786440 | tf_op jit(solution)/shard_map/ppermute | solution.py:18
  55.2 11.2 %copy-start.7 = (f32[512]{0:T(512)S(1)}, f32[512]{0:T(512)}, u32[]{:S(2)}) copy-start(f32[512]{0:T(512)} %param.11) | copy-start | bytes 6148
  55.2 11.2 %copy-start.8 = (f32[256]{0:T(256)S(1)}, f32[256]{0:T(256)}, u32[]{:S(2)}) copy-start(f32[256]{0:T(256)} %param.10) | copy-start | bytes 3076

commit v3 on v1

v3 whole, which is shorter than its diff:
```python
import jax
import jax.numpy as jnp
from jax import lax
from jax.experimental import pallas as pl
from jax.experimental.pallas import tpu as pltpu
from jax.sharding import PartitionSpec as P

SCALE = 64.0
SENT = (1, 0, 3, 4)
LIMIT = 52 * 2**20


def shifted(block, axis, distance):
    devices = range(lax.axis_size(axis))
    route = [(i - distance, i) for i in devices if i - distance in devices]
    return lax.ppermute(block, axis, route)


def terms_kernel(mask_ref, amps_ref, blocks_ref, wide_ref, *rest):
    out_refs, (held, in_sems, out_sems) = rest[:4], rest[4:]
    loads = [
        pltpu.make_async_copy(blocks_ref.at[0, k], held.at[i], in_sems.at[i])
        for i, k in enumerate(SENT)
    ]
    copies = [
        pltpu.make_async_copy(amps_ref, wide_ref.at[i], out_sems.at[i])
        for i in range(wide_ref.shape[0])
    ]
    for load in loads:
        load.start()
    for copy in copies:
        copy.start()
    for i, k in enumerate(SENT):
        loads[i].wait()
        flag = mask_ref[0, k].astype(jnp.float32) * SCALE
        out_refs[i][...] = flag * jnp.dot(
            amps_ref[...], held[i], preferred_element_type=jnp.float32
        )
    for copy in copies:
        copy.wait()


def terms(mask, amps, integrals, chips):
    rows, tile = amps.shape
    whole = pl.BlockSpec(memory_space=pltpu.VMEM)
    product = jax.ShapeDtypeStruct((rows, tile), jnp.float32)
    return pl.pallas_call(
        terms_kernel,
        out_shape=(jax.ShapeDtypeStruct((chips, rows, tile), amps.dtype), *(product,) * 4),
        in_specs=[pl.BlockSpec(memory_space=pltpu.SMEM), whole, pl.BlockSpec(memory_space=pl.ANY)],
        out_specs=(pl.BlockSpec(memory_space=pl.ANY), *(whole,) * 4),
        scratch_shapes=[
            pltpu.VMEM((4, tile, tile), amps.dtype),
            pltpu.SemaphoreType.DMA((4,)),
            pltpu.SemaphoreType.DMA((chips,)),
        ],
        compiler_params=pltpu.CompilerParams(vmem_limit_bytes=LIMIT),
        cost_estimate=pl.CostEstimate(
            flops=8 * rows * tile * tile, bytes_accessed=8 * tile * tile, transcendentals=0
        ),
    )(mask, amps, integrals)


def rest_kernel(mask_ref, amps_ref, blocks_ref, coupling_ref, rows_ref, total_ref, own, held, sems):
    parts, rows = rows_ref.shape[:2]
    load = pltpu.make_async_copy(blocks_ref.at[0, 2], own, sems.at[parts])
    loads = [pltpu.make_async_copy(rows_ref.at[i], held.at[i], sems.at[i]) for i in range(parts)]
    load.start()
    for part in loads:
        part.start()
    load.wait()
    flag = mask_ref[0, 2].astype(jnp.float32)
    total = flag * jnp.dot(amps_ref[...], own[...], preferred_element_type=jnp.float32)
    for i in range(parts):
        loads[i].wait()
        total += jnp.dot(
            coupling_ref[:, i * rows : (i + 1) * rows], held[i], preferred_element_type=jnp.float32
        )
    total_ref[...] = total


def rest_of(mask, amps, integrals, coupling, gathered):
    rows, tile = amps.shape
    whole, there = pl.BlockSpec(memory_space=pltpu.VMEM), pl.BlockSpec(memory_space=pl.ANY)
    return pl.pallas_call(
        rest_kernel,
        out_shape=jax.ShapeDtypeStruct((rows, tile), jnp.float32),
        in_specs=[pl.BlockSpec(memory_space=pltpu.SMEM), whole, there, whole, there],
        out_specs=whole,
        scratch_shapes=[
            pltpu.VMEM((tile, tile), amps.dtype),
            pltpu.VMEM(gathered.shape, amps.dtype),
            pltpu.SemaphoreType.DMA((gathered.shape[0] + 1,)),
        ],
        compiler_params=pltpu.CompilerParams(vmem_limit_bytes=LIMIT),
        cost_estimate=pl.CostEstimate(
            flops=2 * (coupling.size + amps.size) * tile,
            bytes_accessed=2 * (coupling.size + gathered.size),
            transcendentals=0,
        ),
    )(mask, amps, integrals, coupling, gathered)


def body(amps, integrals, mask, pair_coupling, occ_energy, vir_energy):
    wide, *products = terms(mask, amps, integrals, lax.axis_size("occ"))
    gathered = lax.all_to_all(wide, "occ", 0, 0)
    arrived = [
        shifted(products[i].astype(jnp.float16), "vir", (1, 2, -1, -2)[i]) for i in (3, 2, 1, 0)
    ]
    total = rest_of(mask, amps, integrals, pair_coupling, gathered)
    total = total + sum(a.astype(jnp.float32) for a in arrived) * (1.0 / SCALE)
    return total / (occ_energy[:, None] - vir_energy[None, :])


def solution(mesh):
    placed = (
        P("occ", "vir"),
        P("vir", None, None, None),
        P("vir", None),
        P("occ", None),
        P("occ"),
        P("vir"),
    )
    return jax.shard_map(
        body, mesh=mesh, in_specs=placed, out_specs=P("occ", "vir"), check_vma=False
    )
```

time: 63.8 us -> 55.2 us (0.87)
  the two profiles are of different devices: /device:TPU:58 before, /device:TPU:1 now
where the time goes in v3:
time: 55.2 us; the launch traced here: 54.9 us
  starting transfers between devices  23.7 us (43%)
  waiting for transfers between devices  20.9 us (38%)
  Pallas kernels  7.29 us (13%)
  local copies, waits for them, and re-layouts  1.63 us (3%)
  other arithmetic  1.18 us (2%)
    all_to_all x1, waiting for transfers between devices, body(): gathered = lax.all_to_all(wide, 'occ', 0, 0)  20.9 us
    all_to_all x1, starting transfers between devices, body(): gathered = lax.all_to_all(wide, 'occ', 0, 0)  18.4 us
    ppermute x4, starting transfers between devices, shifted(): return lax.ppermute(block, axis, route)  5.33 us
    pallas_call x1, Pallas kernels, terms(): pl.pallas_call(terms_kernel, out_shape=(jax.ShapeDtypeStruct((chips, rows...  4.32 us
    pallas_call x1, Pallas kernels, rest_of(): pl.pallas_call(rest_kernel, out_shape=jax.ShapeDtypeStruct((rows, tile),...  2.98 us
    unnamed x16, local copies, waits for them, and re-layouts  1.63 us
  transfers between devices with their start and end apart: 5, of which 1 were waited for; matrix products, arithmetic and copies ran while one was open for 0% of the time, Pallas kernels for 5%

profile of v3, /device:TPU:1, one launch (start us, length us, event | category | flops | bytes accessed | tf_op | source)
XLA Modules:
  0.0 54.9 jit_solution(8267433573237074416)
XLA Ops:
  0.0 0.0 copy-start.1
  0.0 0.9 %copy-done.1 = bf16[256,512]{1,0:T(8,128)(2,1)S(1)} copy-done((bf16[256,512]{1,0:T(8,128)(2,1)S(1)}, bf16[256,512]{1,0:T(8,128)(2,1)}, u32[]{:S(2)}) %copy-start.1) | copy-done | bytes 262168
  1.0 0.0 copy-start.3
  1.0 0.7 %copy-done.3 = s32[1,5]{1,0:T(1,128)S(1)} copy-done((s32[1,5]{1,0:T(1,128)S(1)}, s32[1,5]{1,0:T(1,128)}, u32[]{:S(2)}) %copy-start.3) | copy-done | bytes 44
  1.6 4.3 %shard_map.64 = (bf16[8,256,512]{2,1,0:T(8,128)(2,1)}, f32[256,512]{1,0:T(8,128)S(1)}, f32[256,512]{1,0:T(8,128)S(1)}, f32[256,512]{1,0:T(8,128)S(1)}, f32[256,512]{1,0:T(8,128)}) custom-call(s32[1,5]{1,0:T(1,128)S(1)} %copy-done.3, bf16[256,512]{1,0:T(8,128)(2,1)S(1)} %copy-done.1, bf16[1,5,512,512]{3,2,1,0:T(8,128)(2,1)} %blocks_ref.3), custom_call_target="tpu_custom_call" | custom-call | flops 536870912 | bytes 2097152 | tf_op jit(solution)/shard_map/pallas_call | solution.py:47
  5.9 18.4 %all-to-all-start = ((bf16[8,256,512]{2,1,0:T(8,128)(2,1)}), bf16[8,256,512]{2,1,0:T(8,128)(2,1)}, u32[]{:S(2)}, u32[]{:S(2)}) async-start(bf16[8,256,512]{2,1,0:T(8,128)(2,1)} %get-tuple-element.10), calls=%async_computation | async-start | bytes 4194304 | tf_op jit(solution)/shard_map/all_to_all | solution.py:106
  24.3 0.0 copy-start.5
  24.3 0.0 copy-start
  24.3 0.0 copy-start.2
  24.3 0.0 copy-start.4
  24.4 1.4 %collective-permute-start.3 = (f16[256,512]{1,0:T(8,128)(2,1)S(1)}, f16[256,512]{1,0:T(8,128)(2,1)S(1)}, u32[]{:S(2)}, u32[]{:S(2)}) collective-permute-start(f16[256,512]{1,0:T(8,128)(2,1)S(1)} %convert_element_type.30), channel_id=1, source_target_pairs={{0,1},{1,2},{2,3},{3,4},{4,5},{5,6},{6,7},{7,8},{8,9},{9,10},{10,1... | collective-permute-start | bytes 786440 | tf_op jit(solution)/shard_map/ppermute | solution.py:16
  25.9 1.3 %collective-permute-start.2 = (f16[256,512]{1,0:T(8,128)(2,1)S(1)}, f16[256,512]{1,0:T(8,128)(2,1)S(1)}, u32[]{:S(2)}, u32[]{:S(2)}) collective-permute-start(f16[256,512]{1,0:T(8,128)(2,1)S(1)} %convert_element_type.28), channel_id=1, source_target_pairs={{0,2},{1,3},{2,4},{3,5},{4,6},{5,7},{6,8},{7,9},{8,10},{9,11},{10,... | collective-permute-start | bytes 786440 | tf_op jit(solution)/shard_map/ppermute | solution.py:16
  27.2 1.3 %collective-permute-start.1 = (f16[256,512]{1,0:T(8,128)(2,1)S(1)}, f16[256,512]{1,0:T(8,128)(2,1)S(1)}, u32[]{:S(2)}, u32[]{:S(2)}) collective-permute-start(f16[256,512]{1,0:T(8,128)(2,1)S(1)} %convert_element_type.26), channel_id=1, source_target_pairs={{1,0},{2,1},{3,2},{4,3},{5,4},{6,5},{7,6},{8,7},{9,8},{10,9},{11,1... | collective-permute-start | bytes 786440 | tf_op jit(solution)/shard_map/ppermute | solution.py:16
  28.5 0.0 copy-done.5
  28.6 0.0 copy-start.6
  28.6 0.0 copy-start.7
  28.6 1.3 %collective-permute-start = (f16[256,512]{1,0:T(8,128)(2,1)S(1)}, f16[256,512]{1,0:T(8,128)(2,1)S(1)}, u32[]{:S(2)}, u32[]{:S(2)}) collective-permute-start(f16[256,512]{1,0:T(8,128)(2,1)S(1)} %convert_element_type.24), channel_id=1, source_target_pairs={{2,0},{3,1},{4,2},{5,3},{6,4},{7,5},{8,6},{9,7},{10,8},{11,9},{12,... | collective-permute-start | bytes 786440 | tf_op jit(solution)/shard_map/ppermute | solution.py:16
  29.9 20.9 %all-to-all-done.rows_ref = bf16[8,256,512]{2,1,0:T(8,128)(2,1)} async-done(((bf16[8,256,512]{2,1,0:T(8,128)(2,1)}), bf16[8,256,512]{2,1,0:T(8,128)(2,1)}, u32[]{:S(2)}, u32[]{:S(2)}) %all-to-all-start) | async-done | bytes 2097184 | tf_op jit(solution)/shard_map/all_to_all | solution.py:106
  50.8 0.0 copy-done
  50.8 0.0 copy-done.2
  50.8 0.0 copy-done.4
  50.8 3.0 %shard_map.65 = f32[256,512]{1,0:T(8,128)S(1)} custom-call(s32[1,5]{1,0:T(1,128)S(1)} %copy-done.4, bf16[256,512]{1,0:T(8,128)(2,1)S(1)} %copy-done.2, bf16[1,5,512,512]{3,2,1,0:T(8,128)(2,1)} %blocks_ref.3, bf16[256,2048]{1,0:T(8,128)(2,1)S(1)} %copy-done, bf16[8,256,512]{2,1,0:T(8,128)(2,1)} %all-to-all-done.rows_ref), custom_call_target="tpu_custom_call" | custom-call | flops 671088640 | bytes 3145728 | tf_op jit(solution)/shard_map/pallas_call | solution.py:85
  53.8 0.0 collective-permute-done.3
  53.8 0.0 collective-permute-done.2
  53.8 0.0 collective-permute-done.1
  53.8 0.0 collective-permute-done
  53.8 0.0 copy-done.6
  53.8 0.0 copy-done.7
  53.8 1.0 %subtract_divide_fusion = f32[256,512]{1,0:T(8,128)} fusion(f32[256,512]{1,0:T(8,128)S(1)} %shard_map.65, f16[256,512]{1,0:T(8,128)(2,1)S(1)} %collective-permute-done.3, f16[256,512]{1,0:T(8,128)(2,1)S(1)} %collective-permute-done.2, f16[256,512]{1,0:T(8,128)(2,1)S(1)} %collective-permute-done.1, f16[256,512]{1,0:T(8,128)(2,1)S(1)} %collective-permute-done, ...), kind=kLoop, calls=%fused_computation | loop fusion | flops 1441792 | bytes 2100224 | tf_op jit(solution)/shard_map/div | solution.py:112
  (4 shorter events, 0.2 us)
Async XLA Ops:
  0.0 0.9 %copy-start.1 = (bf16[256,512]{1,0:T(8,128)(2,1)S(1)}, bf16[256,512]{1,0:T(8,128)(2,1)}, u32[]{:S(2)}) copy-start(bf16[256,512]{1,0:T(8,128)(2,1)} %amps_ref.3) | copy-start | bytes 786436
  1.0 0.7 %copy-start.3 = (s32[1,5]{1,0:T(1,128)S(1)}, s32[1,5]{1,0:T(1,128)}, u32[]{:S(2)}) copy-start(s32[1,5]{1,0:T(1,128)} %mask_ref.3) | copy-start | bytes 64
  5.9 44.8 %all-to-all-start = ((bf16[8,256,512]{2,1,0:T(8,128)(2,1)}), bf16[8,256,512]{2,1,0:T(8,128)(2,1)}, u32[]{:S(2)}, u32[]{:S(2)}) async-start(bf16[8,256,512]{2,1,0:T(8,128)(2,1)} %get-tuple-element.10), calls=%async_computation | async-start | bytes 4194304 | tf_op jit(solution)/shard_map/all_to_all | solution.py:106
  24.3 4.2 %copy-start.5 = (f32[256,512]{1,0:T(8,128)S(1)}, f32[256,512]{1,0:T(8,128)}, u32[]{:S(2)}) copy-start(f32[256,512]{1,0:T(8,128)} %get-tuple-element.11) | copy-start | bytes 1572868
  24.3 26.5 %copy-start = (bf16[256,2048]{1,0:T(8,128)(2,1)S(1)}, bf16[256,2048]{1,0:T(8,128)(2,1)}, u32[]{:S(2)}) copy-start(bf16[256,2048]{1,0:T(8,128)(2,1)} %coupling_ref.1) | copy-start | bytes 3145732
  24.3 26.5 %copy-start.2 = (bf16[256,512]{1,0:T(8,128)(2,1)S(1)}, bf16[256,512]{1,0:T(8,128)(2,1)}, u32[]{:S(2)}) copy-start(bf16[256,512]{1,0:T(8,128)(2,1)} %amps_ref.3) | copy-start | bytes 786436
  24.3 26.5 %copy-start.4 = (s32[1,5]{1,0:T(1,128)S(1)}, s32[1,5]{1,0:T(1,128)}, u32[]{:S(2)}) copy-start(s32[1,5]{1,0:T(1,128)} %mask_ref.3) | copy-start | bytes 64
  24.4 29.4 %collective-permute-start.3 = (f16[256,512]{1,0:T(8,128)(2,1)S(1)}, f16[256,512]{1,0:T(8,128)(2,1)S(1)}, u32[]{:S(2)}, u32[]{:S(2)}) collective-permute-start(f16[256,512]{1,0:T(8,128)(2,1)S(1)} %convert_element_type.30), channel_id=1, source_target_pairs={{0,1},{1,2},{2,3},{3,4},{4,5},{5,6},{6,7},{7,8},{8,9},{9,10},{10,1... | collective-permute-start | bytes 786440 | tf_op jit(solution)/shard_map/ppermute | solution.py:16
  25.9 27.9 %collective-permute-start.2 = (f16[256,512]{1,0:T(8,128)(2,1)S(1)}, f16[256,512]{1,0:T(8,128)(2,1)S(1)}, u32[]{:S(2)}, u32[]{:S(2)}) collective-permute-start(f16[256,512]{1,0:T(8,128)(2,1)S(1)} %convert_element_type.28), channel_id=1, source_target_pairs={{0,2},{1,3},{2,4},{3,5},{4,6},{5,7},{6,8},{7,9},{8,10},{9,11},{10,... | collective-permute-start | bytes 786440 | tf_op jit(solution)/shard_map/ppermute | solution.py:16
  27.2 26.6 %collective-permute-start.1 = (f16[256,512]{1,0:T(8,128)(2,1)S(1)}, f16[256,512]{1,0:T(8,128)(2,1)S(1)}, u32[]{:S(2)}, u32[]{:S(2)}) collective-permute-start(f16[256,512]{1,0:T(8,128)(2,1)S(1)} %convert_element_type.26), channel_id=1, source_target_pairs={{1,0},{2,1},{3,2},{4,3},{5,4},{6,5},{7,6},{8,7},{9,8},{10,9},{11,1... | collective-permute-start | bytes 786440 | tf_op jit(solution)/shard_map/ppermute | solution.py:16
  28.6 25.2 %copy-start.6 = (f32[512]{0:T(512)S(1)}, f32[512]{0:T(512)}, u32[]{:S(2)}) copy-start(f32[512]{0:T(512)} %param.11) | copy-start | bytes 6148
  28.6 25.2 %copy-start.7 = (f32[256]{0:T(256)S(1)}, f32[256]{0:T(256)}, u32[]{:S(2)}) copy-start(f32[256]{0:T(256)} %param.10) | copy-start | bytes 3076
  28.6 25.2 %collective-permute-start = (f16[256,512]{1,0:T(8,128)(2,1)S(1)}, f16[256,512]{1,0:T(8,128)(2,1)S(1)}, u32[]{:S(2)}, u32[]{:S(2)}) collective-permute-start(f16[256,512]{1,0:T(8,128)(2,1)S(1)} %convert_element_type.24), channel_id=1, source_target_pairs={{2,0},{3,1},{4,2},{5,3},{6,4},{7,5},{8,6},{9,7},{10,8},{11,9},{12,... | collective-permute-start | bytes 786440 | tf_op jit(solution)/shard_map/ppermute | solution.py:16

commit v4 on v1

v4 whole, which is shorter than its diff:
```python
import jax
import jax.numpy as jnp
from jax import lax
from jax.experimental import pallas as pl
from jax.experimental.pallas import tpu as pltpu
from jax.sharding import PartitionSpec as P

SCALE = 64.0
OWN = 2
ORDER = (0, 4, 1, 3, OWN)
LIMIT = 51 * 2**20


def shifted(block, axis, distance):
    devices = range(lax.axis_size(axis))
    route = [(i - distance, i) for i in devices if i - distance in devices]
    return lax.ppermute(block, axis, route)


def repeat_kernel(amps_ref, wide_ref, sems):
    copies = [
        pltpu.make_async_copy(amps_ref, wide_ref.at[i], sems.at[i])
        for i in range(wide_ref.shape[0])
    ]
    for copy in copies:
        copy.start()
    for copy in copies:
        copy.wait()


def repeated(amps, times):
    there = pl.BlockSpec(memory_space=pl.ANY)
    return pl.pallas_call(
        repeat_kernel,
        out_shape=jax.ShapeDtypeStruct((times, *amps.shape), amps.dtype),
        in_specs=[there],
        out_specs=there,
        scratch_shapes=[pltpu.SemaphoreType.DMA((times,))],
        compiler_params=pltpu.CompilerParams(vmem_limit_bytes=54 * 2**20),
        cost_estimate=pl.CostEstimate(flops=0, bytes_accessed=2 * times * amps.size, transcendentals=0),
    )(amps)


def terms_kernel(mask_ref, amps_ref, blocks_ref, *rest):
    out_refs, (held, sems) = rest[:5], rest[5:]
    loads = [
        pltpu.make_async_copy(blocks_ref.at[0, k], held.at[i], sems.at[i])
        for i, k in enumerate(ORDER)
    ]
    for load in loads:
        load.start()
    for i, k in enumerate(ORDER):
        loads[i].wait()
        flag = mask_ref[0, k].astype(jnp.float32) * (1.0 if k == OWN else SCALE)
        out_refs[i][...] = flag * jnp.dot(
            amps_ref[...], held[i], preferred_element_type=jnp.float32
        )


def terms(mask, amps, integrals):
    rows, tile = amps.shape
    whole = pl.BlockSpec(memory_space=pltpu.VMEM)
    return pl.pallas_call(
        terms_kernel,
        out_shape=(jax.ShapeDtypeStruct((rows, tile), jnp.float32),) * 5,
        in_specs=[pl.BlockSpec(memory_space=pltpu.SMEM), whole, pl.BlockSpec(memory_space=pl.ANY)],
        out_specs=(whole,) * 5,
        scratch_shapes=[pltpu.VMEM((5, tile, tile), amps.dtype), pltpu.SemaphoreType.DMA((5,))],
        compiler_params=pltpu.CompilerParams(vmem_limit_bytes=LIMIT),
        cost_estimate=pl.CostEstimate(
            flops=10 * rows * tile * tile, bytes_accessed=10 * tile * tile, transcendentals=0
        ),
    )(mask, amps, integrals)


def rest_kernel(coupling_ref, rows_ref, total_ref):
    parts, rows = rows_ref.shape[:2]
    total = jnp.zeros(total_ref.shape, jnp.float32)
    for i in range(parts):
        total += jnp.dot(
            coupling_ref[:, i * rows : (i + 1) * rows], rows_ref[i], preferred_element_type=jnp.float32
        )
    total_ref[...] = total


def rest_of(coupling, gathered):
    whole = pl.BlockSpec(memory_space=pltpu.VMEM)
    return pl.pallas_call(
        rest_kernel,
        out_shape=jax.ShapeDtypeStruct((coupling.shape[0], gathered.shape[2]), jnp.float32),
        in_specs=[whole, whole],
        out_specs=whole,
        compiler_params=pltpu.CompilerParams(vmem_limit_bytes=16 * 2**20),
        cost_estimate=pl.CostEstimate(
            flops=2 * coupling.size * gathered.shape[2],
            bytes_accessed=2 * (coupling.size + gathered.size),
            transcendentals=0,
        ),
    )(coupling, gathered)


def body(amps, integrals, mask, pair_coupling, occ_energy, vir_energy):
    gathered = lax.all_to_all(repeated(amps, lax.axis_size("occ")), "occ", 0, 0)
    *products, own = terms(mask, amps, integrals)
    arrived = [
        shifted(products[i].astype(jnp.float16), "vir", OWN - ORDER[i]) for i in (3, 2, 1, 0)
    ]
    total = rest_of(pair_coupling, gathered) + own
    total = total + sum(a.astype(jnp.float32) for a in arrived) * (1.0 / SCALE)
    return total / (occ_energy[:, None] - vir_energy[None, :])


def solution(mesh):
    placed = (
        P("occ", "vir"),
        P("vir", None, None, None),
        P("vir", None),
        P("occ", None),
        P("occ"),
        P("vir"),
    )
    return jax.shard_map(
        body, mesh=mesh, in_specs=placed, out_specs=P("occ", "vir"), check_vma=False
    )
```

time: 63.8 us -> 115 us (1.80)
  the two profiles are of different devices: /device:TPU:58 before, /device:TPU:24 now
where the time goes in v4:
time: 115 us
  Pallas kernels  68.5 us (60%)
  starting transfers between devices  33.7 us (29%)
  waiting for transfers between devices  7.58 us (7%)
  other arithmetic  4.48 us (4%)
    pallas_call x1, Pallas kernels, repeated(): pl.pallas_call(repeat_kernel, out_shape=jax.ShapeDtypeStruct((times, *amp...  64.7 us
    ppermute x4, starting transfers between devices, shifted(): return lax.ppermute(block, axis, route)  29.3 us
    ppermute x4, waiting for transfers between devices, shifted(): return lax.ppermute(block, axis, route)  7.58 us
    all_to_all x1, starting transfers between devices, body(): gathered = lax.all_to_all(repeated(amps, lax.axis_size('occ')), 'occ', 0, 0)  4.44 us
    pallas_call x1, Pallas kernels, terms(): pl.pallas_call(terms_kernel, out_shape=(jax.ShapeDtypeStruct((rows, tile)...  3.14 us
  transfers between devices with their start and end apart: 5, of which 3 were waited for; matrix products, arithmetic and copies ran while one was open for 2% of the time, Pallas kernels for 3%

profile of v4, /device:TPU:24, one launch (start us, length us, event | category | flops | bytes accessed | tf_op | source)
XLA Modules:
  0.0 114.5 jit_solution(2122248642829405224)
XLA Ops:
  0.0 64.7 %shard_map.64 = bf16[8,256,512]{2,1,0:T(8,128)(2,1)} custom-call(bf16[256,512]{1,0:T(8,128)(2,1)} %amps_ref.3), custom_call_target="tpu_custom_call" | custom-call | bytes 2097152 | tf_op jit(solution)/shard_map/pallas_call | solution.py:33
  64.7 0.0 copy-start.1
  64.7 0.0 copy-start.4
  64.7 4.4 %all-to-all-start = ((bf16[8,256,512]{2,1,0:T(8,128)(2,1)}), bf16[8,256,512]{2,1,0:T(8,128)(2,1)S(1)}, u32[]{:S(2)}, u32[]{:S(2)}) async-start(bf16[8,256,512]{2,1,0:T(8,128)(2,1)} %shard_map.64), calls=%async_computation | async-start | bytes 4194304 | tf_op jit(solution)/shard_map/all_to_all | solution.py:103
  69.2 0.0 copy-done.1
  69.2 0.0 copy-done.4
  69.2 3.1 %shard_map.66 = (f32[256,512]{1,0:T(8,128)S(1)}, f32[256,512]{1,0:T(8,128)S(1)}, f32[256,512]{1,0:T(8,128)S(1)}, f32[256,512]{1,0:T(8,128)S(1)}, f32[256,512]{1,0:T(8,128)S(1)}) custom-call(s32[1,5]{1,0:T(1,128)S(1)} %copy-done.4, bf16[256,512]{1,0:T(8,128)(2,1)S(1)} %copy-done.1, bf16[1,5,512,512]{3,2,1,0:T(8,128)(2,1)} %blocks_ref.1), custom_call_target="tpu_custom_call" | custom-call | flops 671088640 | bytes 2621440 | tf_op jit(solution)/shard_map/pallas_call | solution.py:63
  72.3 0.0 copy-start.2
  72.4 0.0 copy-start
  72.4 5.3 %collective-permute-start.3 = (f16[256,512]{1,0:T(8,128)(2,1)S(1)}, f16[256,512]{1,0:T(8,128)(2,1)}, u32[]{:S(2)}, u32[]{:S(2)}) collective-permute-start(f16[256,512]{1,0:T(8,128)(2,1)S(1)} %convert_element_type.30), channel_id=1, source_target_pairs={{0,2},{1,3},{2,4},{3,5},{4,6},{5,7},{6,8},{7,9},{8,10},{9,11},{10,... | collective-permute-start | bytes 786440 | tf_op jit(solution)/shard_map/ppermute | solution.py:17
  77.7 0.7 convert_element_type.28
  78.5 16.0 %collective-permute-start.2 = (f16[256,512]{1,0:T(8,128)(2,1)}, f16[256,512]{1,0:T(8,128)(2,1)}, u32[]{:S(2)}, u32[]{:S(2)}) collective-permute-start(f16[256,512]{1,0:T(8,128)(2,1)} %convert_element_type.28), channel_id=1, source_target_pairs={{2,0},{3,1},{4,2},{5,3},{6,4},{7,5},{8,6},{9,7},{10,8},{11,9},{12,... | collective-permute-start | bytes 786440 | tf_op jit(solution)/shard_map/ppermute | solution.py:17
  94.5 0.7 convert_element_type.26
  95.3 2.9 %collective-permute-start.1 = (f16[256,512]{1,0:T(8,128)(2,1)}, f16[256,512]{1,0:T(8,128)(2,1)}, u32[]{:S(2)}, u32[]{:S(2)}) collective-permute-start(f16[256,512]{1,0:T(8,128)(2,1)} %convert_element_type.26), channel_id=1, source_target_pairs={{0,1},{1,2},{2,3},{3,4},{4,5},{5,6},{6,7},{7,8},{8,9},{9,10},{10,1... | collective-permute-start | bytes 786440 | tf_op jit(solution)/shard_map/ppermute | solution.py:17
  98.2 0.0 copy-start.5
  98.2 0.0 copy-start.6
  98.2 0.8 convert_element_type.24
  99.0 0.0 copy-done.2
  99.0 5.0 %collective-permute-start = (f16[256,512]{1,0:T(8,128)(2,1)}, f16[256,512]{1,0:T(8,128)(2,1)}, u32[]{:S(2)}, u32[]{:S(2)}) collective-permute-start(f16[256,512]{1,0:T(8,128)(2,1)} %convert_element_type.24), channel_id=1, source_target_pairs={{1,0},{2,1},{3,2},{4,3},{5,4},{6,5},{7,6},{8,7},{9,8},{10,9},{11,1... | collective-permute-start | bytes 786440 | tf_op jit(solution)/shard_map/ppermute | solution.py:17
  104.0 0.0 all-to-all-done.rows_ref
  104.0 0.0 copy-done
  104.0 0.0 copy-start.3
  104.0 0.7 shard_map.65
  104.7 0.0 collective-permute-done.3
  104.7 2.4 %collective-permute-done.2 = f16[256,512]{1,0:T(8,128)(2,1)} collective-permute-done((f16[256,512]{1,0:T(8,128)(2,1)}, f16[256,512]{1,0:T(8,128)(2,1)}, u32[]{:S(2)}, u32[]{:S(2)}) %collective-permute-start.2) | collective-permute-done | bytes 262176 | tf_op jit(solution)/shard_map/ppermute | solution.py:17
  107.1 2.6 %collective-permute-done.1 = f16[256,512]{1,0:T(8,128)(2,1)} collective-permute-done((f16[256,512]{1,0:T(8,128)(2,1)}, f16[256,512]{1,0:T(8,128)(2,1)}, u32[]{:S(2)}, u32[]{:S(2)}) %collective-permute-start.1) | collective-permute-done | bytes 262176 | tf_op jit(solution)/shard_map/ppermute | solution.py:17
  109.7 2.6 %collective-permute-done = f16[256,512]{1,0:T(8,128)(2,1)} collective-permute-done((f16[256,512]{1,0:T(8,128)(2,1)}, f16[256,512]{1,0:T(8,128)(2,1)}, u32[]{:S(2)}, u32[]{:S(2)}) %collective-permute-start) | collective-permute-done | bytes 262176 | tf_op jit(solution)/shard_map/ppermute | solution.py:17
  112.3 0.0 copy-done.5
  112.3 0.0 copy-done.6
  112.3 0.0 copy-done.3
  112.3 2.2 %subtract_divide_fusion = f32[256,512]{1,0:T(8,128)} fusion(f16[256,512]{1,0:T(8,128)(2,1)} %collective-permute-done.3, f16[256,512]{1,0:T(8,128)(2,1)} %collective-permute-done.2, f16[256,512]{1,0:T(8,128)(2,1)} %collective-permute-done.1, f16[256,512]{1,0:T(8,128)(2,1)} %collective-permute-done, f32[256,512]{1,0:T(8,128)S(1)} %shard_map.65, ...), kind=kLoop, calls=%fused_computation | loop fusion | flops 1572864 | bytes 2624512 | tf_op jit(solution)/shard_map/div | solution.py:110
  (1 shorter events, 0.0 us)
Async XLA Ops:
  64.7 4.5 %copy-start.1 = (bf16[256,512]{1,0:T(8,128)(2,1)S(1)}, bf16[256,512]{1,0:T(8,128)(2,1)}, u32[]{:S(2)}) copy-start(bf16[256,512]{1,0:T(8,128)(2,1)} %amps_ref.3) | copy-start | bytes 786436
  64.7 4.5 %copy-start.4 = (s32[1,5]{1,0:T(1,128)S(1)}, s32[1,5]{1,0:T(1,128)}, u32[]{:S(2)}) copy-start(s32[1,5]{1,0:T(1,128)} %mask_ref.1) | copy-start | bytes 64
  64.7 39.3 %all-to-all-start = ((bf16[8,256,512]{2,1,0:T(8,128)(2,1)}), bf16[8,256,512]{2,1,0:T(8,128)(2,1)S(1)}, u32[]{:S(2)}, u32[]{:S(2)}) async-start(bf16[8,256,512]{2,1,0:T(8,128)(2,1)} %shard_map.64), calls=%async_computation | async-start | bytes 4194304 | tf_op jit(solution)/shard_map/all_to_all | solution.py:103
  72.3 26.6 %copy-start.2 = (f32[256,512]{1,0:T(8,128)}, f32[256,512]{1,0:T(8,128)S(1)}, u32[]{:S(2)}) copy-start(f32[256,512]{1,0:T(8,128)S(1)} %get-tuple-element.10) | copy-start | bytes 1572868
  72.4 31.6 %copy-start = (bf16[256,2048]{1,0:T(8,128)(2,1)S(1)}, bf16[256,2048]{1,0:T(8,128)(2,1)}, u32[]{:S(2)}) copy-start(bf16[256,2048]{1,0:T(8,128)(2,1)} %coupling_ref.1) | copy-start | bytes 3145732
  72.4 32.3 %collective-permute-start.3 = (f16[256,512]{1,0:T(8,128)(2,1)S(1)}, f16[256,512]{1,0:T(8,128)(2,1)}, u32[]{:S(2)}, u32[]{:S(2)}) collective-permute-start(f16[256,512]{1,0:T(8,128)(2,1)S(1)} %convert_element_type.30), channel_id=1, source_target_pairs={{0,2},{1,3},{2,4},{3,5},{4,6},{5,7},{6,8},{7,9},{8,10},{9,11},{10,... | collective-permute-start | bytes 786440 | tf_op jit(solution)/shard_map/ppermute | solution.py:17
  78.5 28.6 %collective-permute-start.2 = (f16[256,512]{1,0:T(8,128)(2,1)}, f16[256,512]{1,0:T(8,128)(2,1)}, u32[]{:S(2)}, u32[]{:S(2)}) collective-permute-start(f16[256,512]{1,0:T(8,128)(2,1)} %convert_element_type.28), channel_id=1, source_target_pairs={{2,0},{3,1},{4,2},{5,3},{6,4},{7,5},{8,6},{9,7},{10,8},{11,9},{12,... | collective-permute-start | bytes 786440 | tf_op jit(solution)/shard_map/ppermute | solution.py:17
  95.3 14.5 %collective-permute-start.1 = (f16[256,512]{1,0:T(8,128)(2,1)}, f16[256,512]{1,0:T(8,128)(2,1)}, u32[]{:S(2)}, u32[]{:S(2)}) collective-permute-start(f16[256,512]{1,0:T(8,128)(2,1)} %convert_element_type.26), channel_id=1, source_target_pairs={{0,1},{1,2},{2,3},{3,4},{4,5},{5,6},{6,7},{7,8},{8,9},{9,10},{10,1... | collective-permute-start | bytes 786440 | tf_op jit(solution)/shard_map/ppermute | solution.py:17
  98.2 14.1 %copy-start.5 = (f32[512]{0:T(512)S(1)}, f32[512]{0:T(512)}, u32[]{:S(2)}) copy-start(f32[512]{0:T(512)} %param.11) | copy-start | bytes 6148
  98.2 14.1 %copy-start.6 = (f32[256]{0:T(256)S(1)}, f32[256]{0:T(256)}, u32[]{:S(2)}) copy-start(f32[256]{0:T(256)} %param.10) | copy-start | bytes 3076
  99.0 13.3 %collective-permute-start = (f16[256,512]{1,0:T(8,128)(2,1)}, f16[256,512]{1,0:T(8,128)(2,1)}, u32[]{:S(2)}, u32[]{:S(2)}) collective-permute-start(f16[256,512]{1,0:T(8,128)(2,1)} %convert_element_type.24), channel_id=1, source_target_pairs={{1,0},{2,1},{3,2},{4,3},{5,4},{6,5},{7,6},{8,7},{9,8},{10,9},{11,1... | collective-permute-start | bytes 786440 | tf_op jit(solution)/shard_map/ppermute | solution.py:17
  104.0 8.3 %copy-start.3 = (f32[256,512]{1,0:T(8,128)S(1)}, f32[256,512]{1,0:T(8,128)}, u32[]{:S(2)}) copy-start(f32[256,512]{1,0:T(8,128)} %copy-done.2) | copy-start | bytes 1572868

commit v5 on v4

--- a/solution.py
+++ b/solution.py
@@ -8,7 +8,7 @@
 SCALE = 64.0
 OWN = 2
 ORDER = (0, 4, 1, 3, OWN)
-LIMIT = 51 * 2**20
+LIMIT = 50 * 2**20
 
 
 def shifted(block, axis, distance):
@@ -17,11 +17,12 @@
     return lax.ppermute(block, axis, route)
 
 
-def repeat_kernel(amps_ref, wide_ref, sems):
-    copies = [
-        pltpu.make_async_copy(amps_ref, wide_ref.at[i], sems.at[i])
-        for i in range(wide_ref.shape[0])
-    ]
+def repeat_kernel(amps_ref, wide_ref, held, sems):
+    times = wide_ref.shape[0]
+    load = pltpu.make_async_copy(amps_ref, held, sems.at[times])
+    load.start()
+    load.wait()
+    copies = [pltpu.make_async_copy(held, wide_ref.at[i], sems.at[i]) for i in range(times)]
     for copy in copies:
         copy.start()
     for copy in copies:
@@ -35,7 +36,7 @@
         out_shape=jax.ShapeDtypeStruct((times, *amps.shape), amps.dtype),
         in_specs=[there],
         out_specs=there,
-        scratch_shapes=[pltpu.SemaphoreType.DMA((times,))],
+        scratch_shapes=[pltpu.VMEM(amps.shape, amps.dtype), pltpu.SemaphoreType.DMA((times + 1,))],
         compiler_params=pltpu.CompilerParams(vmem_limit_bytes=54 * 2**20),
         cost_estimate=pl.CostEstimate(flops=0, bytes_accessed=2 * times * amps.size, transcendentals=0),
     )(amps)
@@ -73,24 +74,32 @@
     )(mask, amps, integrals)
 
 
-def rest_kernel(coupling_ref, rows_ref, total_ref):
+def rest_kernel(coupling_ref, rows_ref, total_ref, held, sems):
     parts, rows = rows_ref.shape[:2]
+    loads = [pltpu.make_async_copy(rows_ref.at[i], held.at[i], sems.at[i]) for i in range(parts)]
+    for part in loads:
+        part.start()
     total = jnp.zeros(total_ref.shape, jnp.float32)
     for i in range(parts):
+        loads[i].wait()
         total += jnp.dot(
-            coupling_ref[:, i * rows : (i + 1) * rows], rows_ref[i], preferred_element_type=jnp.float32
+            coupling_ref[:, i * rows : (i + 1) * rows], held[i], preferred_element_type=jnp.float32
         )
     total_ref[...] = total
 
 
 def rest_of(coupling, gathered):
-    whole = pl.BlockSpec(memory_space=pltpu.VMEM)
+    whole, there = pl.BlockSpec(memory_space=pltpu.VMEM), pl.BlockSpec(memory_space=pl.ANY)
     return pl.pallas_call(
         rest_kernel,
         out_shape=jax.ShapeDtypeStruct((coupling.shape[0], gathered.shape[2]), jnp.float32),
-        in_specs=[whole, whole],
+        in_specs=[whole, there],
         out_specs=whole,
-        compiler_params=pltpu.CompilerParams(vmem_limit_bytes=16 * 2**20),
+        scratch_shapes=[
+            pltpu.VMEM(gathered.shape, gathered.dtype),
+            pltpu.SemaphoreType.DMA((gathered.shape[0],)),
+        ],
+        compiler_params=pltpu.CompilerParams(vmem_limit_bytes=52 * 2**20),
         cost_estimate=pl.CostEstimate(
             flops=2 * coupling.size * gathered.shape[2],
             bytes_accessed=2 * (coupling.size + gathered.size),

time: 115 us -> 51.9 us (0.45)
  Pallas kernels: 68.5 us -> 7.56 us
  other arithmetic: 4.48 us -> 2.12 us
    pallas_call x1, Pallas kernels: 64.7 us -> 2.34 us  [repeated(): pl.pallas_call(repeat_kernel, out_shape=jax.ShapeDtypeStruct((times, *amp...]
    convert_element_type x4, other arithmetic: 2.27 us -> 0.15 us  [body(): products[i].astype(jnp.float16)]
    pallas_call x1, Pallas kernels: 0.7 us -> 2.07 us  [rest_of(): pl.pallas_call(rest_kernel, out_shape=jax.ShapeDtypeStruct((coupling.shap...]
  transfers between devices with their start and end apart: 5 -> 5, of which waited for: 3 -> 3; matrix products, arithmetic and copies ran while one was open for 2% -> 0% of each run, Pallas kernels for 3% -> 10%
where the time goes in v5:
time: 51.9 us; the launch traced here: 50.9 us
  starting transfers between devices  33.8 us (65%)
  Pallas kernels  7.56 us (15%)
  waiting for transfers between devices  7.24 us (14%)
  other arithmetic  2.12 us (4%)
    ppermute x4, starting transfers between devices, shifted(): return lax.ppermute(block, axis, route)  29.3 us
    ppermute x4, waiting for transfers between devices, shifted(): return lax.ppermute(block, axis, route)  7.24 us
    all_to_all x1, starting transfers between devices, body(): gathered = lax.all_to_all(repeated(amps, lax.axis_size('occ')), 'occ', 0, 0)  4.5 us
    pallas_call x1, Pallas kernels, terms(): pl.pallas_call(terms_kernel, out_shape=(jax.ShapeDtypeStruct((rows, tile)...  3.14 us
    pallas_call x1, Pallas kernels, repeated(): pl.pallas_call(repeat_kernel, out_shape=jax.ShapeDtypeStruct((times, *amp...  2.34 us
    pallas_call x1, Pallas kernels, rest_of(): pl.pallas_call(rest_kernel, out_shape=jax.ShapeDtypeStruct((coupling.shap...  2.07 us
    div x1, other arithmetic, body(): return total / (occ_energy[:, None] - vir_energy[None, :])  1.97 us
  transfers between devices with their start and end apart: 5, of which 3 were waited for; matrix products, arithmetic and copies ran while one was open for 0% of the time, Pallas kernels for 10%

profile of v5, /device:TPU:24, one launch (start us, length us, event | category | flops | bytes accessed | tf_op | source)
XLA Modules:
  0.0 50.9 jit_solution(8933136794735533081)
XLA Ops:
  0.0 2.3 %shard_map.64 = bf16[8,256,512]{2,1,0:T(8,128)(2,1)} custom-call(bf16[256,512]{1,0:T(8,128)(2,1)} %amps_ref.3), custom_call_target="tpu_custom_call" | custom-call | bytes 2097152 | tf_op jit(solution)/shard_map/pallas_call | solution.py:34
  2.4 0.0 copy-start.1
  2.4 0.0 copy-start.2
  2.4 4.5 %all-to-all-start = ((bf16[8,256,512]{2,1,0:T(8,128)(2,1)}), bf16[8,256,512]{2,1,0:T(8,128)(2,1)}, u32[]{:S(2)}, u32[]{:S(2)}) async-start(bf16[8,256,512]{2,1,0:T(8,128)(2,1)} %shard_map.64), calls=%async_computation | async-start | bytes 4194304 | tf_op jit(solution)/shard_map/all_to_all | solution.py:112
  6.9 0.0 copy-done.1
  6.9 0.0 copy-done.2
  6.9 3.1 %shard_map.66 = (f32[256,512]{1,0:T(8,128)S(1)}, f32[256,512]{1,0:T(8,128)S(1)}, f32[256,512]{1,0:T(8,128)S(1)}, f32[256,512]{1,0:T(8,128)S(1)}, f32[256,512]{1,0:T(8,128)S(1)}) custom-call(s32[1,5]{1,0:T(1,128)S(1)} %copy-done.2, bf16[256,512]{1,0:T(8,128)(2,1)S(1)} %copy-done.1, bf16[1,5,512,512]{3,2,1,0:T(8,128)(2,1)} %blocks_ref.1), custom_call_target="tpu_custom_call" | custom-call | flops 671088640 | bytes 2621440 | tf_op jit(solution)/shard_map/pallas_call | solution.py:64
  10.1 0.0 copy-start
  10.1 5.3 %collective-permute-start.3 = (f16[256,512]{1,0:T(8,128)(2,1)S(1)}, f16[256,512]{1,0:T(8,128)(2,1)S(1)}, u32[]{:S(2)}, u32[]{:S(2)}) collective-permute-start(f16[256,512]{1,0:T(8,128)(2,1)S(1)} %convert_element_type.30), channel_id=1, source_target_pairs={{0,2},{1,3},{2,4},{3,5},{4,6},{5,7},{6,8},{7,9},{8,10},{9,11},{10,... | collective-permute-start | bytes 786440 | tf_op jit(solution)/shard_map/ppermute | solution.py:17
  15.5 16.0 %collective-permute-start.2 = (f16[256,512]{1,0:T(8,128)(2,1)S(1)}, f16[256,512]{1,0:T(8,128)(2,1)S(1)}, u32[]{:S(2)}, u32[]{:S(2)}) collective-permute-start(f16[256,512]{1,0:T(8,128)(2,1)S(1)} %convert_element_type.28), channel_id=1, source_target_pairs={{2,0},{3,1},{4,2},{5,3},{6,4},{7,5},{8,6},{9,7},{10,8},{11,9},{12,... | collective-permute-start | bytes 786440 | tf_op jit(solution)/shard_map/ppermute | solution.py:17
  31.6 2.9 %collective-permute-start.1 = (f16[256,512]{1,0:T(8,128)(2,1)S(1)}, f16[256,512]{1,0:T(8,128)(2,1)S(1)}, u32[]{:S(2)}, u32[]{:S(2)}) collective-permute-start(f16[256,512]{1,0:T(8,128)(2,1)S(1)} %convert_element_type.26), channel_id=1, source_target_pairs={{0,1},{1,2},{2,3},{3,4},{4,5},{5,6},{6,7},{7,8},{8,9},{9,10},{10,1... | collective-permute-start | bytes 786440 | tf_op jit(solution)/shard_map/ppermute | solution.py:17
  34.5 0.0 copy-start.3
  34.5 0.0 copy-start.4
  34.6 5.0 %collective-permute-start = (f16[256,512]{1,0:T(8,128)(2,1)S(1)}, f16[256,512]{1,0:T(8,128)(2,1)}, u32[]{:S(2)}, u32[]{:S(2)}) collective-permute-start(f16[256,512]{1,0:T(8,128)(2,1)S(1)} %convert_element_type.24), channel_id=1, source_target_pairs={{1,0},{2,1},{3,2},{4,3},{5,4},{6,5},{7,6},{8,7},{9,8},{10,9},{11,1... | collective-permute-start | bytes 786440 | tf_op jit(solution)/shard_map/ppermute | solution.py:17
  39.6 0.0 all-to-all-done.rows_ref
  39.6 0.0 copy-done
  39.6 2.1 %shard_map.65 = f32[256,512]{1,0:T(8,128)S(1)} custom-call(bf16[256,2048]{1,0:T(8,128)(2,1)S(1)} %copy-done, bf16[8,256,512]{2,1,0:T(8,128)(2,1)} %all-to-all-done.rows_ref), custom_call_target="tpu_custom_call" | custom-call | flops 536870912 | bytes 3145728 | tf_op jit(solution)/shard_map/pallas_call | solution.py:93
  41.7 0.0 collective-permute-done.3
  41.7 2.1 %collective-permute-done.2 = f16[256,512]{1,0:T(8,128)(2,1)S(1)} collective-permute-done((f16[256,512]{1,0:T(8,128)(2,1)S(1)}, f16[256,512]{1,0:T(8,128)(2,1)S(1)}, u32[]{:S(2)}, u32[]{:S(2)}) %collective-permute-start.2) | collective-permute-done | bytes 262176 | tf_op jit(solution)/shard_map/ppermute | solution.py:17
  43.8 3.4 %collective-permute-done.1 = f16[256,512]{1,0:T(8,128)(2,1)S(1)} collective-permute-done((f16[256,512]{1,0:T(8,128)(2,1)S(1)}, f16[256,512]{1,0:T(8,128)(2,1)S(1)}, u32[]{:S(2)}, u32[]{:S(2)}) %collective-permute-start.1) | collective-permute-done | bytes 262176 | tf_op jit(solution)/shard_map/ppermute | solution.py:17
  47.2 1.7 %collective-permute-done = f16[256,512]{1,0:T(8,128)(2,1)} collective-permute-done((f16[256,512]{1,0:T(8,128)(2,1)S(1)}, f16[256,512]{1,0:T(8,128)(2,1)}, u32[]{:S(2)}, u32[]{:S(2)}) %collective-permute-start) | collective-permute-done | bytes 262176 | tf_op jit(solution)/shard_map/ppermute | solution.py:17
  49.0 0.0 copy-done.3
  49.0 0.0 copy-done.4
  49.0 2.0 %subtract_divide_fusion = f32[256,512]{1,0:T(8,128)} fusion(f16[256,512]{1,0:T(8,128)(2,1)S(1)} %collective-permute-done.3, f16[256,512]{1,0:T(8,128)(2,1)S(1)} %collective-permute-done.2, f16[256,512]{1,0:T(8,128)(2,1)S(1)} %collective-permute-done.1, f16[256,512]{1,0:T(8,128)(2,1)} %collective-permute-done, f32[256,512]{1,0:T(8,128)S(1)} %shard_map.65, ...), kind=kLoop, calls=%fused_computation | loop fusion | flops 1572864 | bytes 2624512 | tf_op jit(solution)/shard_map/div | solution.py:119
  (4 shorter events, 0.2 us)
Async XLA Ops:
  2.4 4.5 %copy-start.1 = (bf16[256,512]{1,0:T(8,128)(2,1)S(1)}, bf16[256,512]{1,0:T(8,128)(2,1)}, u32[]{:S(2)}) copy-start(bf16[256,512]{1,0:T(8,128)(2,1)} %amps_ref.3) | copy-start | bytes 786436
  2.4 4.5 %copy-start.2 = (s32[1,5]{1,0:T(1,128)S(1)}, s32[1,5]{1,0:T(1,128)}, u32[]{:S(2)}) copy-start(s32[1,5]{1,0:T(1,128)} %mask_ref.1) | copy-start | bytes 64
  2.4 37.2 %all-to-all-start = ((bf16[8,256,512]{2,1,0:T(8,128)(2,1)}), bf16[8,256,512]{2,1,0:T(8,128)(2,1)}, u32[]{:S(2)}, u32[]{:S(2)}) async-start(bf16[8,256,512]{2,1,0:T(8,128)(2,1)} %shard_map.64), calls=%async_computation | async-start | bytes 4194304 | tf_op jit(solution)/shard_map/all_to_all | solution.py:112
  10.1 29.6 %copy-start = (bf16[256,2048]{1,0:T(8,128)(2,1)S(1)}, bf16[256,2048]{1,0:T(8,128)(2,1)}, u32[]{:S(2)}) copy-start(bf16[256,2048]{1,0:T(8,128)(2,1)} %coupling_ref.1) | copy-start | bytes 3145732
  10.1 31.6 %collective-permute-start.3 = (f16[256,512]{1,0:T(8,128)(2,1)S(1)}, f16[256,512]{1,0:T(8,128)(2,1)S(1)}, u32[]{:S(2)}, u32[]{:S(2)}) collective-permute-start(f16[256,512]{1,0:T(8,128)(2,1)S(1)} %convert_element_type.30), channel_id=1, source_target_pairs={{0,2},{1,3},{2,4},{3,5},{4,6},{5,7},{6,8},{7,9},{8,10},{9,11},{10,... | collective-permute-start | bytes 786440 | tf_op jit(solution)/shard_map/ppermute | solution.py:17
  15.5 28.3 %collective-permute-start.2 = (f16[256,512]{1,0:T(8,128)(2,1)S(1)}, f16[256,512]{1,0:T(8,128)(2,1)S(1)}, u32[]{:S(2)}, u32[]{:S(2)}) collective-permute-start(f16[256,512]{1,0:T(8,128)(2,1)S(1)} %convert_element_type.28), channel_id=1, source_target_pairs={{2,0},{3,1},{4,2},{5,3},{6,4},{7,5},{8,6},{9,7},{10,8},{11,9},{12,... | collective-permute-start | bytes 786440 | tf_op jit(solution)/shard_map/ppermute | solution.py:17
  31.6 15.7 %collective-permute-start.1 = (f16[256,512]{1,0:T(8,128)(2,1)S(1)}, f16[256,512]{1,0:T(8,128)(2,1)S(1)}, u32[]{:S(2)}, u32[]{:S(2)}) collective-permute-start(f16[256,512]{1,0:T(8,128)(2,1)S(1)} %convert_element_type.26), channel_id=1, source_target_pairs={{0,1},{1,2},{2,3},{3,4},{4,5},{5,6},{6,7},{7,8},{8,9},{9,10},{10,1... | collective-permute-start | bytes 786440 | tf_op jit(solution)/shard_map/ppermute | solution.py:17
  34.5 14.5 %copy-start.3 = (f32[512]{0:T(512)S(1)}, f32[512]{0:T(512)}, u32[]{:S(2)}) copy-start(f32[512]{0:T(512)} %param.11) | copy-start | bytes 6148
  34.5 14.4 %copy-start.4 = (f32[256]{0:T(256)S(1)}, f32[256]{0:T(256)}, u32[]{:S(2)}) copy-start(f32[256]{0:T(256)} %param.10) | copy-start | bytes 3076
  34.6 14.4 %collective-permute-start = (f16[256,512]{1,0:T(8,128)(2,1)S(1)}, f16[256,512]{1,0:T(8,128)(2,1)}, u32[]{:S(2)}, u32[]{:S(2)}) collective-permute-start(f16[256,512]{1,0:T(8,128)(2,1)S(1)} %convert_element_type.24), channel_id=1, source_target_pairs={{1,0},{2,1},{3,2},{4,3},{5,4},{6,5},{7,6},{8,7},{9,8},{10,9},{11,1... | collective-permute-start | bytes 786440 | tf_op jit(solution)/shard_map/ppermute | solution.py:17

commit v6 on v5

--- a/solution.py
+++ b/solution.py
@@ -1,3 +1,5 @@
+import functools
+
 import jax
 import jax.numpy as jnp
 from jax import lax
@@ -8,7 +10,10 @@
 SCALE = 64.0
 OWN = 2
 ORDER = (0, 4, 1, 3, OWN)
-LIMIT = 50 * 2**20
+LIMIT = 48 * 2**20
+HALF_LIMIT = 8 * 2**20
+CORES = 2
+NEAR_WORK = 64
 
 
 def shifted(block, axis, distance):
@@ -74,60 +79,63 @@
     )(mask, amps, integrals)
 
 
-def rest_kernel(coupling_ref, rows_ref, total_ref, held, sems):
-    parts, rows = rows_ref.shape[:2]
-    loads = [pltpu.make_async_copy(rows_ref.at[i], held.at[i], sems.at[i]) for i in range(parts)]
-    for part in loads:
-        part.start()
-    total = jnp.zeros(total_ref.shape, jnp.float32)
-    for i in range(parts):
-        loads[i].wait()
+def columns_of(coupling_ref, chip, core, rows):
+    start = pl.multiple_of((CORES * chip + core) * rows, rows)
+    return coupling_ref[:, pl.ds(start, rows)]
+
+
+def half_kernel(flip, coupling_ref, rows_ref, before_ref, total_ref):
+    core = lax.axis_index("core")
+    core = CORES - 1 - core if flip else core
+    chips, rows = rows_ref.shape[:2]
+    total = before_ref[...]
+    for chip in range(chips):
         total += jnp.dot(
-            coupling_ref[:, i * rows : (i + 1) * rows], held[i], preferred_element_type=jnp.float32
+            columns_of(coupling_ref, chip, core, rows), rows_ref[chip], preferred_element_type=jnp.float32
         )
     total_ref[...] = total
 
 
-def rest_of(coupling, gathered):
-    whole, there = pl.BlockSpec(memory_space=pltpu.VMEM), pl.BlockSpec(memory_space=pl.ANY)
+def half_of(coupling, gathered, before, flip, flops):
+    whole = pl.BlockSpec(memory_space=pltpu.VMEM)
     return pl.pallas_call(
-        rest_kernel,
-        out_shape=jax.ShapeDtypeStruct((coupling.shape[0], gathered.shape[2]), jnp.float32),
-        in_specs=[whole, there],
+        functools.partial(half_kernel, flip),
+        out_shape=jax.ShapeDtypeStruct(before.shape, jnp.float32),
+        in_specs=[whole] * 3,
         out_specs=whole,
-        scratch_shapes=[
-            pltpu.VMEM(gathered.shape, gathered.dtype),
-            pltpu.SemaphoreType.DMA((gathered.shape[0],)),
-        ],
-        compiler_params=pltpu.CompilerParams(vmem_limit_bytes=52 * 2**20),
+        compiler_params=pltpu.CompilerParams(vmem_limit_bytes=HALF_LIMIT),
         cost_estimate=pl.CostEstimate(
-            flops=2 * coupling.size * gathered.shape[2],
-            bytes_accessed=2 * (coupling.size + gathered.size),
-            transcendentals=0,
+            flops=flops, bytes_accessed=2 * (coupling.size + gathered.size), transcendentals=0
         ),
-    )(coupling, gathered)
+    )(coupling, gathered, before)
 
 
 def body(amps, integrals, mask, pair_coupling, occ_energy, vir_energy):
-    gathered = lax.all_to_all(repeated(amps, lax.axis_size("occ")), "occ", 0, 0)
+    near = lax.all_to_all(repeated(amps, lax.axis_size("x")), "x", 0, 0)
     *products, own = terms(mask, amps, integrals)
     arrived = [
-        shifted(products[i].astype(jnp.float16), "vir", OWN - ORDER[i]) for i in (3, 2, 1, 0)
+        shifted(products[i].astype(jnp.float16), "vir", OWN - ORDER[i]) for i in (0, 1, 2, 3)
     ]
-    total = rest_of(pair_coupling, gathered) + own
+    far = lax.ppermute(near, "core", [(i, CORES - 1 - i) for i in range(CORES)])
+    work = pair_coupling.size * amps.shape[1]
+    total = half_of(pair_coupling, near, own, False, NEAR_WORK * work)
+    total = half_of(pair_coupling, far, total, True, work)
     total = total + sum(a.astype(jnp.float32) for a in arrived) * (1.0 / SCALE)
     return total / (occ_energy[:, None] - vir_energy[None, :])
 
 
 def solution(mesh):
+    devices = mesh.devices.reshape(-1, CORES, mesh.shape["vir"])
+    lines = jax.sharding.Mesh(devices, ("x", "core", "vir"))
+    occ = ("x", "core")
     placed = (
-        P("occ", "vir"),
+        P(occ, "vir"),
         P("vir", None, None, None),
         P("vir", None),
-        P("occ", None),
-        P("occ"),
+        P(occ, None),
+        P(occ),
         P("vir"),
     )
     return jax.shard_map(
-        body, mesh=mesh, in_specs=placed, out_specs=P("occ", "vir"), check_vma=False
+        body, mesh=lines, in_specs=placed, out_specs=P(occ, "vir"), check_vma=False
     )

time: 51.9 us -> 48.7 us (0.938)
  waiting for transfers between devices: 7.24 us -> 4.05 us
  starting transfers between devices: 33.8 us -> 35.5 us
  Pallas kernels: 7.56 us -> 6.53 us
    ppermute x4, waiting for transfers between devices: 7.24 us -> 2.92 us  [shifted(): return lax.ppermute(block, axis, route)]
    ppermute x0 -> x1, starting transfers between devices: none -> 1.92 us  [body(): far = lax.ppermute(near, 'core', [(i, CORES - 1 - i) for i in range(CORES)])]
    ppermute x0 -> x1, waiting for transfers between devices: none -> 1.13 us  [body(): far = lax.ppermute(near, 'core', [(i, CORES - 1 - i) for i in range(CORES)])]
    div x1, other arithmetic: 1.97 us -> 1.01 us  [body(): return total / (occ_energy[:, None] - vir_energy[None, :])]
    pallas_call x1, Pallas kernels: 3.14 us -> 2.28 us  [terms(): pl.pallas_call(terms_kernel, out_shape=(jax.ShapeDtypeStruct((rows, tile)...]
    convert_element_type x4, other arithmetic: 0.15 us -> 0.85 us  [body(): products[i].astype(jnp.float16)]
    pallas_call x1 -> x2, Pallas kernels: 2.07 us -> 2.1 us  [half_of(): pl.pallas_call(functools.partial(half_kernel, flip), out_shape=jax.ShapeD...]
  transfers between devices with their start and end apart: 5 -> 6, of which waited for: 3 -> 3; matrix products, arithmetic and copies ran while one was open for 0% -> 2% of each run, Pallas kernels for 10% -> 9%
where the time goes in v6:
time: 48.7 us; the launch traced here: 48.2 us
  starting transfers between devices  35.5 us (73%)
  Pallas kernels  6.53 us (13%)
  waiting for transfers between devices  4.05 us (8%)
  other arithmetic  1.86 us (4%)
    ppermute x4, starting transfers between devices, shifted(): return lax.ppermute(block, axis, route)  29.3 us
    all_to_all x1, starting transfers between devices, body(): near = lax.all_to_all(repeated(amps, lax.axis_size('x')), 'x', 0, 0)  4.3 us
    ppermute x4, waiting for transfers between devices, shifted(): return lax.ppermute(block, axis, route)  2.92 us
    pallas_call x1, Pallas kernels, terms(): pl.pallas_call(terms_kernel, out_shape=(jax.ShapeDtypeStruct((rows, tile)...  2.28 us
    pallas_call x1, Pallas kernels, repeated(): pl.pallas_call(repeat_kernel, out_shape=jax.ShapeDtypeStruct((times, *amp...  2.15 us
    pallas_call x2, Pallas kernels, half_of(): pl.pallas_call(functools.partial(half_kernel, flip), out_shape=jax.ShapeD...  2.1 us
    ppermute x1, starting transfers between devices, body(): far = lax.ppermute(near, 'core', [(i, CORES - 1 - i) for i in range(CORES)])  1.92 us
    ppermute x1, waiting for transfers between devices, body(): far = lax.ppermute(near, 'core', [(i, CORES - 1 - i) for i in range(CORES)])  1.13 us
  transfers between devices with their start and end apart: 6, of which 3 were waited for; matrix products, arithmetic and copies ran while one was open for 2% of the time, Pallas kernels for 9%

profile of v6, /device:TPU:24, one launch (start us, length us, event | category | flops | bytes accessed | tf_op | source)
XLA Modules:
  0.0 48.2 jit_solution(9097066831880693821)
XLA Ops:
  0.0 0.0 copy-start.2
  0.0 0.0 copy-start
  0.0 0.0 copy-start.3
  0.0 2.1 %shard_map.64 = bf16[4,256,512]{2,1,0:T(8,128)(2,1)} custom-call(bf16[256,512]{1,0:T(8,128)(2,1)} %amps_ref.3), custom_call_target="tpu_custom_call" | custom-call | bytes 1048576 | tf_op jit(solution)/shard_map/pallas_call | solution.py:39
  2.2 4.3 %all-to-all-start = ((bf16[4,256,512]{2,1,0:T(8,128)(2,1)}), bf16[4,256,512]{2,1,0:T(8,128)(2,1)}, u32[]{:S(2)}, u32[]{:S(2)}) async-start(bf16[4,256,512]{2,1,0:T(8,128)(2,1)} %shard_map.64), calls=%async_computation | async-start | bytes 2097152 | tf_op jit(solution)/shard_map/all_to_all | solution.py:114
  6.5 0.0 copy-done.2
  6.5 0.0 copy-done
  6.5 0.0 copy-done.3
  6.5 2.3 %shard_map.65 = (f32[256,512]{1,0:T(8,128)S(1)}, f32[256,512]{1,0:T(8,128)S(1)}, f32[256,512]{1,0:T(8,128)S(1)}, f32[256,512]{1,0:T(8,128)S(1)}, f32[256,512]{1,0:T(8,128)S(1)}) custom-call(s32[1,5]{1,0:T(1,128)S(1)} %copy-done.3, bf16[256,512]{1,0:T(8,128)(2,1)S(1)} %copy-done.2, bf16[1,5,512,512]{3,2,1,0:T(8,128)(2,1)S(1)} %copy-done), custom_call_target="tpu_custom_call" | custom-call | flops 671088640 | bytes 2621440 | tf_op jit(solution)/shard_map/pallas_call | solution.py:69
  8.8 0.0 copy-start.1
  8.8 5.3 %collective-permute-start.1 = (f16[256,512]{1,0:T(8,128)(2,1)S(1)}, f16[256,512]{1,0:T(8,128)(2,1)S(1)}, u32[]{:S(2)}, u32[]{:S(2)}) collective-permute-start(f16[256,512]{1,0:T(8,128)(2,1)S(1)} %convert_element_type.24), channel_id=1, source_target_pairs={{0,2},{1,3},{2,4},{3,5},{4,6},{5,7},{6,8},{7,9},{8,10},{9,11},{10,... | collective-permute-start | bytes 786440 | tf_op jit(solution)/shard_map/ppermute | solution.py:22
  14.2 16.0 %collective-permute-start.2 = (f16[256,512]{1,0:T(8,128)(2,1)S(1)}, f16[256,512]{1,0:T(8,128)(2,1)S(1)}, u32[]{:S(2)}, u32[]{:S(2)}) collective-permute-start(f16[256,512]{1,0:T(8,128)(2,1)S(1)} %convert_element_type.26), channel_id=1, source_target_pairs={{2,0},{3,1},{4,2},{5,3},{6,4},{7,5},{8,6},{9,7},{10,8},{11,9},{12,... | collective-permute-start | bytes 786440 | tf_op jit(solution)/shard_map/ppermute | solution.py:22
  30.3 2.9 %collective-permute-start.3 = (f16[256,512]{1,0:T(8,128)(2,1)S(1)}, f16[256,512]{1,0:T(8,128)(2,1)S(1)}, u32[]{:S(2)}, u32[]{:S(2)}) collective-permute-start(f16[256,512]{1,0:T(8,128)(2,1)S(1)} %convert_element_type.28), channel_id=1, source_target_pairs={{0,1},{1,2},{2,3},{3,4},{4,5},{5,6},{6,7},{7,8},{8,9},{9,10},{10,1... | collective-permute-start | bytes 786440 | tf_op jit(solution)/shard_map/ppermute | solution.py:22
  33.2 0.7 %convert_element_type.30 = f16[256,512]{1,0:T(8,128)(2,1)} convert(f32[256,512]{1,0:T(8,128)S(1)} %get-tuple-element.14) | non-fusion elementwise | flops 131072 | bytes 786432 | tf_op jit(solution)/shard_map/convert_element_type | solution.py:117
  34.0 5.0 %collective-permute-start.4 = (f16[256,512]{1,0:T(8,128)(2,1)}, f16[256,512]{1,0:T(8,128)(2,1)S(1)}, u32[]{:S(2)}, u32[]{:S(2)}) collective-permute-start(f16[256,512]{1,0:T(8,128)(2,1)} %convert_element_type.30), channel_id=1, source_target_pairs={{1,0},{2,1},{3,2},{4,3},{5,4},{6,5},{7,6},{8,7},{9,8},{10,9},{11,1... | collective-permute-start | bytes 786440 | tf_op jit(solution)/shard_map/ppermute | solution.py:22
  39.0 0.0 all-to-all-done.rows_ref
  39.0 1.9 %collective-permute-start = (bf16[4,256,512]{2,1,0:T(8,128)(2,1)}, bf16[4,256,512]{2,1,0:T(8,128)(2,1)S(1)}, u32[]{:S(2)}, u32[]{:S(2)}) collective-permute-start(bf16[4,256,512]{2,1,0:T(8,128)(2,1)} %all-to-all-done.rows_ref), channel_id=1, source_target_pairs={{0,128},{128,0},{1,129},{129,1},{2,130},{130,2},{3,131},{131,3},{4... | collective-permute-start | bytes 3145736 | tf_op jit(solution)/shard_map/ppermute | solution.py:119
  40.9 0.0 copy-done.1
  40.9 1.7 %shard_map.66.before_ref = f32[256,512]{1,0:T(8,128)S(1)} custom-call(bf16[256,2048]{1,0:T(8,128)(2,1)S(1)} %copy-done.1, bf16[4,256,512]{2,1,0:T(8,128)(2,1)} %all-to-all-done.rows_ref, f32[256,512]{1,0:T(8,128)S(1)} %get-tuple-element.10.before_ref), custom_call_target="tpu_custom_call" | custom-call | flops 17179869184 | bytes 2097152 | tf_op jit(solution)/shard_map/pallas_call | solution.py:101
  42.6 0.0 copy-start.4
  42.6 0.0 copy-start.5
  42.6 1.1 %collective-permute-done.rows_ref = bf16[4,256,512]{2,1,0:T(8,128)(2,1)S(1)} collective-permute-done((bf16[4,256,512]{2,1,0:T(8,128)(2,1)}, bf16[4,256,512]{2,1,0:T(8,128)(2,1)S(1)}, u32[]{:S(2)}, u32[]{:S(2)}) %collective-permute-start) | collective-permute-done | bytes 1048608 | tf_op jit(solution)/shard_map/ppermute | solution.py:119
  43.8 0.4 shard_map.67
  44.2 0.0 collective-permute-done.1
  44.2 0.0 collective-permute-done.2
  44.2 1.1 %collective-permute-done.3 = f16[256,512]{1,0:T(8,128)(2,1)S(1)} collective-permute-done((f16[256,512]{1,0:T(8,128)(2,1)S(1)}, f16[256,512]{1,0:T(8,128)(2,1)S(1)}, u32[]{:S(2)}, u32[]{:S(2)}) %collective-permute-start.3) | collective-permute-done | bytes 262176 | tf_op jit(solution)/shard_map/ppermute | solution.py:22
  45.3 1.8 %collective-permute-done.4 = f16[256,512]{1,0:T(8,128)(2,1)S(1)} collective-permute-done((f16[256,512]{1,0:T(8,128)(2,1)}, f16[256,512]{1,0:T(8,128)(2,1)S(1)}, u32[]{:S(2)}, u32[]{:S(2)}) %collective-permute-start.4) | collective-permute-done | bytes 262176 | tf_op jit(solution)/shard_map/ppermute | solution.py:22
  47.1 0.0 copy-done.4
  47.1 0.0 copy-done.5
  47.1 1.0 %subtract_divide_fusion = f32[256,512]{1,0:T(8,128)} fusion(f32[256,512]{1,0:T(8,128)S(1)} %shard_map.67, f16[256,512]{1,0:T(8,128)(2,1)S(1)} %collective-permute-done.4, f16[256,512]{1,0:T(8,128)(2,1)S(1)} %collective-permute-done.3, f16[256,512]{1,0:T(8,128)(2,1)S(1)} %collective-permute-done.2, f16[256,512]{1,0:T(8,128)(2,1)S(1)} %collective-permute-done.1, ...), kind=kLoop, calls=%fused_computation | loop fusion | flops 1441792 | bytes 2100224 | tf_op jit(solution)/shard_map/div | solution.py:124
  (3 shorter events, 0.1 us)
Async XLA Ops:
  0.0 6.5 %copy-start.2 = (bf16[256,512]{1,0:T(8,128)(2,1)S(1)}, bf16[256,512]{1,0:T(8,128)(2,1)}, u32[]{:S(2)}) copy-start(bf16[256,512]{1,0:T(8,128)(2,1)} %amps_ref.3) | copy-start | bytes 786436
  0.0 6.5 %copy-start = (bf16[1,5,512,512]{3,2,1,0:T(8,128)(2,1)S(1)}, bf16[1,5,512,512]{3,2,1,0:T(8,128)(2,1)}, u32[]{:S(2)}) copy-start(bf16[1,5,512,512]{3,2,1,0:T(8,128)(2,1)} %blocks_ref.1) | copy-start | bytes 7864324
  0.0 6.5 %copy-start.3 = (s32[1,5]{1,0:T(1,128)S(1)}, s32[1,5]{1,0:T(1,128)}, u32[]{:S(2)}) copy-start(s32[1,5]{1,0:T(1,128)} %mask_ref.1) | copy-start | bytes 64
  2.2 36.8 %all-to-all-start = ((bf16[4,256,512]{2,1,0:T(8,128)(2,1)}), bf16[4,256,512]{2,1,0:T(8,128)(2,1)}, u32[]{:S(2)}, u32[]{:S(2)}) async-start(bf16[4,256,512]{2,1,0:T(8,128)(2,1)} %shard_map.64), calls=%async_computation | async-start | bytes 2097152 | tf_op jit(solution)/shard_map/all_to_all | solution.py:114
  8.8 32.2 %copy-start.1 = (bf16[256,2048]{1,0:T(8,128)(2,1)S(1)}, bf16[256,2048]{1,0:T(8,128)(2,1)}, u32[]{:S(2)}) copy-start(bf16[256,2048]{1,0:T(8,128)(2,1)} %coupling_ref.3) | copy-start | bytes 3145732
  8.8 35.4 %collective-permute-start.1 = (f16[256,512]{1,0:T(8,128)(2,1)S(1)}, f16[256,512]{1,0:T(8,128)(2,1)S(1)}, u32[]{:S(2)}, u32[]{:S(2)}) collective-permute-start(f16[256,512]{1,0:T(8,128)(2,1)S(1)} %convert_element_type.24), channel_id=1, source_target_pairs={{0,2},{1,3},{2,4},{3,5},{4,6},{5,7},{6,8},{7,9},{8,10},{9,11},{10,... | collective-permute-start | bytes 786440 | tf_op jit(solution)/shard_map/ppermute | solution.py:22
  14.2 30.0 %collective-permute-start.2 = (f16[256,512]{1,0:T(8,128)(2,1)S(1)}, f16[256,512]{1,0:T(8,128)(2,1)S(1)}, u32[]{:S(2)}, u32[]{:S(2)}) collective-permute-start(f16[256,512]{1,0:T(8,128)(2,1)S(1)} %convert_element_type.26), channel_id=1, source_target_pairs={{2,0},{3,1},{4,2},{5,3},{6,4},{7,5},{8,6},{9,7},{10,8},{11,9},{12,... | collective-permute-start | bytes 786440 | tf_op jit(solution)/shard_map/ppermute | solution.py:22
  30.3 15.0 %collective-permute-start.3 = (f16[256,512]{1,0:T(8,128)(2,1)S(1)}, f16[256,512]{1,0:T(8,128)(2,1)S(1)}, u32[]{:S(2)}, u32[]{:S(2)}) collective-permute-start(f16[256,512]{1,0:T(8,128)(2,1)S(1)} %convert_element_type.28), channel_id=1, source_target_pairs={{0,1},{1,2},{2,3},{3,4},{4,5},{5,6},{6,7},{7,8},{8,9},{9,10},{10,1... | collective-permute-start | bytes 786440 | tf_op jit(solution)/shard_map/ppermute | solution.py:22
  34.0 13.2 %collective-permute-start.4 = (f16[256,512]{1,0:T(8,128)(2,1)}, f16[256,512]{1,0:T(8,128)(2,1)S(1)}, u32[]{:S(2)}, u32[]{:S(2)}) collective-permute-start(f16[256,512]{1,0:T(8,128)(2,1)} %convert_element_type.30), channel_id=1, source_target_pairs={{1,0},{2,1},{3,2},{4,3},{5,4},{6,5},{7,6},{8,7},{9,8},{10,9},{11,1... | collective-permute-start | bytes 786440 | tf_op jit(solution)/shard_map/ppermute | solution.py:22
  39.0 4.8 %collective-permute-start = (bf16[4,256,512]{2,1,0:T(8,128)(2,1)}, bf16[4,256,512]{2,1,0:T(8,128)(2,1)S(1)}, u32[]{:S(2)}, u32[]{:S(2)}) collective-permute-start(bf16[4,256,512]{2,1,0:T(8,128)(2,1)} %all-to-all-done.rows_ref), channel_id=1, source_target_pairs={{0,128},{128,0},{1,129},{129,1},{2,130},{130,2},{3,131},{131,3},{4... | collective-permute-start | bytes 3145736 | tf_op jit(solution)/shard_map/ppermute | solution.py:119
  42.6 4.5 %copy-start.4 = (f32[512]{0:T(512)S(1)}, f32[512]{0:T(512)}, u32[]{:S(2)}) copy-start(f32[512]{0:T(512)} %param.11) | copy-start | bytes 6148
  42.6 4.5 %copy-start.5 = (f32[256]{0:T(256)S(1)}, f32[256]{0:T(256)}, u32[]{:S(2)}) copy-start(f32[256]{0:T(256)} %param.10) | copy-start | bytes 3076

commit v7 on v6

--- a/solution.py
+++ b/solution.py
@@ -20,31 +20,6 @@
     devices = range(lax.axis_size(axis))
     route = [(i - distance, i) for i in devices if i - distance in devices]
     return lax.ppermute(block, axis, route)
-
-
-def repeat_kernel(amps_ref, wide_ref, held, sems):
-    times = wide_ref.shape[0]
-    load = pltpu.make_async_copy(amps_ref, held, sems.at[times])
-    load.start()
-    load.wait()
-    copies = [pltpu.make_async_copy(held, wide_ref.at[i], sems.at[i]) for i in range(times)]
-    for copy in copies:
-        copy.start()
-    for copy in copies:
-        copy.wait()
-
-
-def repeated(amps, times):
-    there = pl.BlockSpec(memory_space=pl.ANY)
-    return pl.pallas_call(
-        repeat_kernel,
-        out_shape=jax.ShapeDtypeStruct((times, *amps.shape), amps.dtype),
-        in_specs=[there],
-        out_specs=there,
-        scratch_shapes=[pltpu.VMEM(amps.shape, amps.dtype), pltpu.SemaphoreType.DMA((times + 1,))],
-        compiler_params=pltpu.CompilerParams(vmem_limit_bytes=54 * 2**20),
-        cost_estimate=pl.CostEstimate(flops=0, bytes_accessed=2 * times * amps.size, transcendentals=0),
-    )(amps)
 
 
 def terms_kernel(mask_ref, amps_ref, blocks_ref, *rest):
@@ -111,7 +86,8 @@
 
 
 def body(amps, integrals, mask, pair_coupling, occ_energy, vir_energy):
-    near = lax.all_to_all(repeated(amps, lax.axis_size("x")), "x", 0, 0)
+    wide = jnp.broadcast_to(amps[None], (lax.axis_size("x"), *amps.shape))
+    near = lax.all_to_all(wide, "x", 0, 0)
     *products, own = terms(mask, amps, integrals)
     arrived = [
         shifted(products[i].astype(jnp.float16), "vir", OWN - ORDER[i]) for i in (0, 1, 2, 3)

time: 48.7 us -> 48.7 us (level)
  local copies, waits for them, and re-layouts: 0.03 us -> 2.21 us
  Pallas kernels: 6.53 us -> 4.38 us
    broadcast_in_dim x0 -> x1, local copies, waits for them, and re-layouts: none -> 2.18 us  [body(): wide = jnp.broadcast_to(amps[None], (lax.axis_size('x'), *amps.shape))]
    pallas_call x1 -> x0, Pallas kernels: 2.15 us -> none  [repeated(): pl.pallas_call(repeat_kernel, out_shape=jax.ShapeDtypeStruct((times, *amp...]
where the time goes in v7:
time: 48.7 us; the launch traced here: 48.2 us
  starting transfers between devices  35.5 us (73%)
  Pallas kernels  4.38 us (9%)
  waiting for transfers between devices  4.06 us (8%)
  local copies, waits for them, and re-layouts  2.21 us (5%)
  other arithmetic  1.86 us (4%)
    ppermute x4, starting transfers between devices, shifted(): return lax.ppermute(block, axis, route)  29.3 us
    all_to_all x1, starting transfers between devices, body(): near = lax.all_to_all(wide, 'x', 0, 0)  4.29 us
    ppermute x4, waiting for transfers between devices, shifted(): return lax.ppermute(block, axis, route)  2.92 us
    pallas_call x1, Pallas kernels, terms(): pl.pallas_call(terms_kernel, out_shape=(jax.ShapeDtypeStruct((rows, tile)...  2.28 us
    broadcast_in_dim x1, local copies, waits for them, and re-layouts, body(): wide = jnp.broadcast_to(amps[None], (lax.axis_size('x'), *amps.shape))  2.18 us
    pallas_call x2, Pallas kernels, half_of(): pl.pallas_call(functools.partial(half_kernel, flip), out_shape=jax.ShapeD...  2.1 us
    ppermute x1, starting transfers between devices, body(): far = lax.ppermute(near, 'core', [(i, CORES - 1 - i) for i in range(CORES)])  1.92 us
    ppermute x1, waiting for transfers between devices, body(): far = lax.ppermute(near, 'core', [(i, CORES - 1 - i) for i in range(CORES)])  1.13 us
  transfers between devices with their start and end apart: 6, of which 3 were waited for; matrix products, arithmetic and copies ran while one was open for 2% of the time, Pallas kernels for 9%

profile of v7, /device:TPU:24, one launch (start us, length us, event | category | flops | bytes accessed | tf_op | source)
XLA Modules:
  0.0 48.2 jit_solution(16536624828542572502)
XLA Ops:
  0.0 0.0 copy-start.2
  0.0 0.0 copy-start
  0.0 0.0 copy-start.3
  0.0 2.2 %broadcast_in_dim.2 = bf16[4,256,512]{2,1,0:T(8,128)(2,1)} broadcast(bf16[256,512]{1,0:T(8,128)(2,1)} %amps_ref.1), dimensions={1,2} | broadcast | bytes 1310720 | tf_op jit(solution)/shard_map/broadcast_in_dim | solution.py:89
  2.2 4.3 %all-to-all-start = ((bf16[4,256,512]{2,1,0:T(8,128)(2,1)}), bf16[4,256,512]{2,1,0:T(8,128)(2,1)}, u32[]{:S(2)}, u32[]{:S(2)}) async-start(bf16[4,256,512]{2,1,0:T(8,128)(2,1)} %broadcast_in_dim.2), calls=%async_computation | async-start | bytes 2097152 | tf_op jit(solution)/shard_map/all_to_all | solution.py:90
  6.5 0.0 copy-done.2
  6.5 0.0 copy-done
  6.5 0.0 copy-done.3
  6.5 2.3 %shard_map.64 = (f32[256,512]{1,0:T(8,128)S(1)}, f32[256,512]{1,0:T(8,128)S(1)}, f32[256,512]{1,0:T(8,128)S(1)}, f32[256,512]{1,0:T(8,128)S(1)}, f32[256,512]{1,0:T(8,128)S(1)}) custom-call(s32[1,5]{1,0:T(1,128)S(1)} %copy-done.3, bf16[256,512]{1,0:T(8,128)(2,1)S(1)} %copy-done.2, bf16[1,5,512,512]{3,2,1,0:T(8,128)(2,1)S(1)} %copy-done), custom_call_target="tpu_custom_call" | custom-call | flops 671088640 | bytes 2621440 | tf_op jit(solution)/shard_map/pallas_call | solution.py:44
  8.8 0.0 copy-start.1
  8.8 5.3 %collective-permute-start.1 = (f16[256,512]{1,0:T(8,128)(2,1)S(1)}, f16[256,512]{1,0:T(8,128)(2,1)S(1)}, u32[]{:S(2)}, u32[]{:S(2)}) collective-permute-start(f16[256,512]{1,0:T(8,128)(2,1)S(1)} %convert_element_type.24), channel_id=1, source_target_pairs={{0,2},{1,3},{2,4},{3,5},{4,6},{5,7},{6,8},{7,9},{8,10},{9,11},{10,... | collective-permute-start | bytes 786440 | tf_op jit(solution)/shard_map/ppermute | solution.py:22
  14.2 16.0 %collective-permute-start.2 = (f16[256,512]{1,0:T(8,128)(2,1)S(1)}, f16[256,512]{1,0:T(8,128)(2,1)S(1)}, u32[]{:S(2)}, u32[]{:S(2)}) collective-permute-start(f16[256,512]{1,0:T(8,128)(2,1)S(1)} %convert_element_type.26), channel_id=1, source_target_pairs={{2,0},{3,1},{4,2},{5,3},{6,4},{7,5},{8,6},{9,7},{10,8},{11,9},{12,... | collective-permute-start | bytes 786440 | tf_op jit(solution)/shard_map/ppermute | solution.py:22
  30.3 2.9 %collective-permute-start.3 = (f16[256,512]{1,0:T(8,128)(2,1)S(1)}, f16[256,512]{1,0:T(8,128)(2,1)S(1)}, u32[]{:S(2)}, u32[]{:S(2)}) collective-permute-start(f16[256,512]{1,0:T(8,128)(2,1)S(1)} %convert_element_type.28), channel_id=1, source_target_pairs={{0,1},{1,2},{2,3},{3,4},{4,5},{5,6},{6,7},{7,8},{8,9},{9,10},{10,1... | collective-permute-start | bytes 786440 | tf_op jit(solution)/shard_map/ppermute | solution.py:22
  33.2 0.7 %convert_element_type.30 = f16[256,512]{1,0:T(8,128)(2,1)} convert(f32[256,512]{1,0:T(8,128)S(1)} %get-tuple-element.14) | non-fusion elementwise | flops 131072 | bytes 786432 | tf_op jit(solution)/shard_map/convert_element_type | solution.py:93
  34.0 5.0 %collective-permute-start.4 = (f16[256,512]{1,0:T(8,128)(2,1)}, f16[256,512]{1,0:T(8,128)(2,1)S(1)}, u32[]{:S(2)}, u32[]{:S(2)}) collective-permute-start(f16[256,512]{1,0:T(8,128)(2,1)} %convert_element_type.30), channel_id=1, source_target_pairs={{1,0},{2,1},{3,2},{4,3},{5,4},{6,5},{7,6},{8,7},{9,8},{10,9},{11,1... | collective-permute-start | bytes 786440 | tf_op jit(solution)/shard_map/ppermute | solution.py:22
  39.0 0.0 all-to-all-done.rows_ref
  39.0 1.9 %collective-permute-start = (bf16[4,256,512]{2,1,0:T(8,128)(2,1)}, bf16[4,256,512]{2,1,0:T(8,128)(2,1)S(1)}, u32[]{:S(2)}, u32[]{:S(2)}) collective-permute-start(bf16[4,256,512]{2,1,0:T(8,128)(2,1)} %all-to-all-done.rows_ref), channel_id=1, source_target_pairs={{0,128},{128,0},{1,129},{129,1},{2,130},{130,2},{3,131},{131,3},{4... | collective-permute-start | bytes 3145736 | tf_op jit(solution)/shard_map/ppermute | solution.py:95
  40.9 0.0 copy-done.1
  41.0 1.7 %shard_map.65.before_ref = f32[256,512]{1,0:T(8,128)S(1)} custom-call(bf16[256,2048]{1,0:T(8,128)(2,1)S(1)} %copy-done.1, bf16[4,256,512]{2,1,0:T(8,128)(2,1)} %all-to-all-done.rows_ref, f32[256,512]{1,0:T(8,128)S(1)} %get-tuple-element.10.before_ref), custom_call_target="tpu_custom_call" | custom-call | flops 17179869184 | bytes 2097152 | tf_op jit(solution)/shard_map/pallas_call | solution.py:76
  42.6 0.0 copy-start.4
  42.6 0.0 copy-start.5
  42.6 1.1 %collective-permute-done.rows_ref = bf16[4,256,512]{2,1,0:T(8,128)(2,1)S(1)} collective-permute-done((bf16[4,256,512]{2,1,0:T(8,128)(2,1)}, bf16[4,256,512]{2,1,0:T(8,128)(2,1)S(1)}, u32[]{:S(2)}, u32[]{:S(2)}) %collective-permute-start) | collective-permute-done | bytes 1048608 | tf_op jit(solution)/shard_map/ppermute | solution.py:95
  43.8 0.4 shard_map.66
  44.2 0.0 collective-permute-done.1
  44.2 0.0 collective-permute-done.2
  44.2 1.1 %collective-permute-done.3 = f16[256,512]{1,0:T(8,128)(2,1)S(1)} collective-permute-done((f16[256,512]{1,0:T(8,128)(2,1)S(1)}, f16[256,512]{1,0:T(8,128)(2,1)S(1)}, u32[]{:S(2)}, u32[]{:S(2)}) %collective-permute-start.3) | collective-permute-done | bytes 262176 | tf_op jit(solution)/shard_map/ppermute | solution.py:22
  45.3 1.8 %collective-permute-done.4 = f16[256,512]{1,0:T(8,128)(2,1)S(1)} collective-permute-done((f16[256,512]{1,0:T(8,128)(2,1)}, f16[256,512]{1,0:T(8,128)(2,1)S(1)}, u32[]{:S(2)}, u32[]{:S(2)}) %collective-permute-start.4) | collective-permute-done | bytes 262176 | tf_op jit(solution)/shard_map/ppermute | solution.py:22
  47.2 0.0 copy-done.4
  47.2 0.0 copy-done.5
  47.2 1.0 %subtract_divide_fusion = f32[256,512]{1,0:T(8,128)} fusion(f32[256,512]{1,0:T(8,128)S(1)} %shard_map.66, f16[256,512]{1,0:T(8,128)(2,1)S(1)} %collective-permute-done.4, f16[256,512]{1,0:T(8,128)(2,1)S(1)} %collective-permute-done.3, f16[256,512]{1,0:T(8,128)(2,1)S(1)} %collective-permute-done.2, f16[256,512]{1,0:T(8,128)(2,1)S(1)} %collective-permute-done.1, ...), kind=kLoop, calls=%fused_computation | loop fusion | flops 1441792 | bytes 2100224 | tf_op jit(solution)/shard_map/div | solution.py:100
  (3 shorter events, 0.1 us)
Async XLA Ops:
  0.0 6.5 %copy-start.2 = (bf16[256,512]{1,0:T(8,128)(2,1)S(1)}, bf16[256,512]{1,0:T(8,128)(2,1)}, u32[]{:S(2)}) copy-start(bf16[256,512]{1,0:T(8,128)(2,1)} %amps_ref.1) | copy-start | bytes 786436
  0.0 6.5 %copy-start = (bf16[1,5,512,512]{3,2,1,0:T(8,128)(2,1)S(1)}, bf16[1,5,512,512]{3,2,1,0:T(8,128)(2,1)}, u32[]{:S(2)}) copy-start(bf16[1,5,512,512]{3,2,1,0:T(8,128)(2,1)} %blocks_ref.1) | copy-start | bytes 7864324
  0.0 6.5 %copy-start.3 = (s32[1,5]{1,0:T(1,128)S(1)}, s32[1,5]{1,0:T(1,128)}, u32[]{:S(2)}) copy-start(s32[1,5]{1,0:T(1,128)} %mask_ref.1) | copy-start | bytes 64
  2.2 36.8 %all-to-all-start = ((bf16[4,256,512]{2,1,0:T(8,128)(2,1)}), bf16[4,256,512]{2,1,0:T(8,128)(2,1)}, u32[]{:S(2)}, u32[]{:S(2)}) async-start(bf16[4,256,512]{2,1,0:T(8,128)(2,1)} %broadcast_in_dim.2), calls=%async_computation | async-start | bytes 2097152 | tf_op jit(solution)/shard_map/all_to_all | solution.py:90
  8.8 32.2 %copy-start.1 = (bf16[256,2048]{1,0:T(8,128)(2,1)S(1)}, bf16[256,2048]{1,0:T(8,128)(2,1)}, u32[]{:S(2)}) copy-start(bf16[256,2048]{1,0:T(8,128)(2,1)} %coupling_ref.3) | copy-start | bytes 3145732
  8.8 35.4 %collective-permute-start.1 = (f16[256,512]{1,0:T(8,128)(2,1)S(1)}, f16[256,512]{1,0:T(8,128)(2,1)S(1)}, u32[]{:S(2)}, u32[]{:S(2)}) collective-permute-start(f16[256,512]{1,0:T(8,128)(2,1)S(1)} %convert_element_type.24), channel_id=1, source_target_pairs={{0,2},{1,3},{2,4},{3,5},{4,6},{5,7},{6,8},{7,9},{8,10},{9,11},{10,... | collective-permute-start | bytes 786440 | tf_op jit(solution)/shard_map/ppermute | solution.py:22
  14.2 30.0 %collective-permute-start.2 = (f16[256,512]{1,0:T(8,128)(2,1)S(1)}, f16[256,512]{1,0:T(8,128)(2,1)S(1)}, u32[]{:S(2)}, u32[]{:S(2)}) collective-permute-start(f16[256,512]{1,0:T(8,128)(2,1)S(1)} %convert_element_type.26), channel_id=1, source_target_pairs={{2,0},{3,1},{4,2},{5,3},{6,4},{7,5},{8,6},{9,7},{10,8},{11,9},{12,... | collective-permute-start | bytes 786440 | tf_op jit(solution)/shard_map/ppermute | solution.py:22
  30.3 15.0 %collective-permute-start.3 = (f16[256,512]{1,0:T(8,128)(2,1)S(1)}, f16[256,512]{1,0:T(8,128)(2,1)S(1)}, u32[]{:S(2)}, u32[]{:S(2)}) collective-permute-start(f16[256,512]{1,0:T(8,128)(2,1)S(1)} %convert_element_type.28), channel_id=1, source_target_pairs={{0,1},{1,2},{2,3},{3,4},{4,5},{5,6},{6,7},{7,8},{8,9},{9,10},{10,1... | collective-permute-start | bytes 786440 | tf_op jit(solution)/shard_map/ppermute | solution.py:22
  34.0 13.2 %collective-permute-start.4 = (f16[256,512]{1,0:T(8,128)(2,1)}, f16[256,512]{1,0:T(8,128)(2,1)S(1)}, u32[]{:S(2)}, u32[]{:S(2)}) collective-permute-start(f16[256,512]{1,0:T(8,128)(2,1)} %convert_element_type.30), channel_id=1, source_target_pairs={{1,0},{2,1},{3,2},{4,3},{5,4},{6,5},{7,6},{8,7},{9,8},{10,9},{11,1... | collective-permute-start | bytes 786440 | tf_op jit(solution)/shard_map/ppermute | solution.py:22
  39.0 4.8 %collective-permute-start = (bf16[4,256,512]{2,1,0:T(8,128)(2,1)}, bf16[4,256,512]{2,1,0:T(8,128)(2,1)S(1)}, u32[]{:S(2)}, u32[]{:S(2)}) collective-permute-start(bf16[4,256,512]{2,1,0:T(8,128)(2,1)} %all-to-all-done.rows_ref), channel_id=1, source_target_pairs={{0,128},{128,0},{1,129},{129,1},{2,130},{130,2},{3,131},{131,3},{4... | collective-permute-start | bytes 3145736 | tf_op jit(solution)/shard_map/ppermute | solution.py:95
  42.6 4.5 %copy-start.4 = (f32[512]{0:T(512)S(1)}, f32[512]{0:T(512)}, u32[]{:S(2)}) copy-start(f32[512]{0:T(512)} %param.11) | copy-start | bytes 6148
  42.6 4.5 %copy-start.5 = (f32[256]{0:T(256)S(1)}, f32[256]{0:T(256)}, u32[]{:S(2)}) copy-start(f32[256]{0:T(256)} %param.10) | copy-start | bytes 3076

commit v8 on v7

--- a/solution.py
+++ b/solution.py
@@ -10,7 +10,7 @@
 SCALE = 64.0
 OWN = 2
 ORDER = (0, 4, 1, 3, OWN)
-LIMIT = 48 * 2**20
+LIMIT = 16 * 2**20
 HALF_LIMIT = 8 * 2**20
 CORES = 2
 NEAR_WORK = 64
@@ -22,19 +22,11 @@
     return lax.ppermute(block, axis, route)
 
 
-def terms_kernel(mask_ref, amps_ref, blocks_ref, *rest):
-    out_refs, (held, sems) = rest[:5], rest[5:]
-    loads = [
-        pltpu.make_async_copy(blocks_ref.at[0, k], held.at[i], sems.at[i])
-        for i, k in enumerate(ORDER)
-    ]
-    for load in loads:
-        load.start()
-    for i, k in enumerate(ORDER):
-        loads[i].wait()
+def terms_kernel(mask_ref, amps_ref, blocks_ref, *out_refs):
+    for k, out_ref in zip(ORDER, out_refs):
         flag = mask_ref[0, k].astype(jnp.float32) * (1.0 if k == OWN else SCALE)
-        out_refs[i][...] = flag * jnp.dot(
-            amps_ref[...], held[i], preferred_element_type=jnp.float32
+        out_ref[...] = flag * jnp.dot(
+            amps_ref[...], blocks_ref[0, k], preferred_element_type=jnp.float32
         )
 
 
@@ -44,9 +36,8 @@
     return pl.pallas_call(
         terms_kernel,
         out_shape=(jax.ShapeDtypeStruct((rows, tile), jnp.float32),) * 5,
-        in_specs=[pl.BlockSpec(memory_space=pltpu.SMEM), whole, pl.BlockSpec(memory_space=pl.ANY)],
+        in_specs=[pl.BlockSpec(memory_space=pltpu.SMEM), whole, whole],
         out_specs=(whole,) * 5,
-        scratch_shapes=[pltpu.VMEM((5, tile, tile), amps.dtype), pltpu.SemaphoreType.DMA((5,))],
         compiler_params=pltpu.CompilerParams(vmem_limit_bytes=LIMIT),
         cost_estimate=pl.CostEstimate(
             flops=10 * rows * tile * tile, bytes_accessed=10 * tile * tile, transcendentals=0

time: 48.7 us -> 47.8 us (0.982)
  Pallas kernels: 4.38 us -> 3.49 us
    pallas_call x1, Pallas kernels: 2.28 us -> 1.39 us  [terms(): pl.pallas_call(terms_kernel, out_shape=(jax.ShapeDtypeStruct((rows, tile)...]
  transfers between devices with their start and end apart: 6 -> 6, of which waited for: 3 -> 3; matrix products, arithmetic and copies ran while one was open for 2% -> 2% of each run, Pallas kernels for 9% -> 7%
where the time goes in v8:
time: 47.8 us; the launch traced here: 47.3 us
  starting transfers between devices  35.5 us (74%)
  waiting for transfers between devices  4.06 us (8%)
  Pallas kernels  3.49 us (7%)
  local copies, waits for them, and re-layouts  2.21 us (5%)
  other arithmetic  1.86 us (4%)
    ppermute x4, starting transfers between devices, shifted(): return lax.ppermute(block, axis, route)  29.3 us
    all_to_all x1, starting transfers between devices, body(): near = lax.all_to_all(wide, 'x', 0, 0)  4.29 us
    ppermute x4, waiting for transfers between devices, shifted(): return lax.ppermute(block, axis, route)  2.92 us
    broadcast_in_dim x1, local copies, waits for them, and re-layouts, body(): wide = jnp.broadcast_to(amps[None], (lax.axis_size('x'), *amps.shape))  2.18 us
    pallas_call x2, Pallas kernels, half_of(): pl.pallas_call(functools.partial(half_kernel, flip), out_shape=jax.ShapeD...  2.1 us
    ppermute x1, starting transfers between devices, body(): far = lax.ppermute(near, 'core', [(i, CORES - 1 - i) for i in range(CORES)])  1.92 us
    pallas_call x1, Pallas kernels, terms(): pl.pallas_call(terms_kernel, out_shape=(jax.ShapeDtypeStruct((rows, tile)...  1.39 us
    ppermute x1, waiting for transfers between devices, body(): far = lax.ppermute(near, 'core', [(i, CORES - 1 - i) for i in range(CORES)])  1.13 us
  transfers between devices with their start and end apart: 6, of which 3 were waited for; matrix products, arithmetic and copies ran while one was open for 2% of the time, Pallas kernels for 7%

profile of v8, /device:TPU:24, one launch (start us, length us, event | category | flops | bytes accessed | tf_op | source)
XLA Modules:
  0.0 47.3 jit_solution(3959248317068340173)
XLA Ops:
  0.0 0.0 copy-start.2
  0.0 0.0 copy-start
  0.0 0.0 copy-start.3
  0.0 2.2 %broadcast_in_dim.2 = bf16[4,256,512]{2,1,0:T(8,128)(2,1)} broadcast(bf16[256,512]{1,0:T(8,128)(2,1)} %amps_ref.1), dimensions={1,2} | broadcast | bytes 1310720 | tf_op jit(solution)/shard_map/broadcast_in_dim | solution.py:80
  2.2 4.3 %all-to-all-start = ((bf16[4,256,512]{2,1,0:T(8,128)(2,1)}), bf16[4,256,512]{2,1,0:T(8,128)(2,1)}, u32[]{:S(2)}, u32[]{:S(2)}) async-start(bf16[4,256,512]{2,1,0:T(8,128)(2,1)} %broadcast_in_dim.2), calls=%async_computation | async-start | bytes 2097152 | tf_op jit(solution)/shard_map/all_to_all | solution.py:81
  6.5 0.0 copy-done.2
  6.5 0.0 copy-done
  6.5 0.0 copy-done.3
  6.5 1.4 %shard_map.64 = (f32[256,512]{1,0:T(8,128)S(1)}, f32[256,512]{1,0:T(8,128)S(1)}, f32[256,512]{1,0:T(8,128)S(1)}, f32[256,512]{1,0:T(8,128)S(1)}, f32[256,512]{1,0:T(8,128)S(1)}) custom-call(s32[1,5]{1,0:T(1,128)S(1)} %copy-done.3, bf16[256,512]{1,0:T(8,128)(2,1)S(1)} %copy-done.2, bf16[1,5,512,512]{3,2,1,0:T(8,128)(2,1)S(1)} %copy-done), custom_call_target="tpu_custom_call" | custom-call | flops 671088640 | bytes 2621440 | tf_op jit(solution)/shard_map/pallas_call | solution.py:36
  7.9 0.0 copy-start.1
  7.9 5.3 %collective-permute-start.1 = (f16[256,512]{1,0:T(8,128)(2,1)S(1)}, f16[256,512]{1,0:T(8,128)(2,1)S(1)}, u32[]{:S(2)}, u32[]{:S(2)}) collective-permute-start(f16[256,512]{1,0:T(8,128)(2,1)S(1)} %convert_element_type.24), channel_id=1, source_target_pairs={{0,2},{1,3},{2,4},{3,5},{4,6},{5,7},{6,8},{7,9},{8,10},{9,11},{10,... | collective-permute-start | bytes 786440 | tf_op jit(solution)/shard_map/ppermute | solution.py:22
  13.3 16.0 %collective-permute-start.2 = (f16[256,512]{1,0:T(8,128)(2,1)S(1)}, f16[256,512]{1,0:T(8,128)(2,1)S(1)}, u32[]{:S(2)}, u32[]{:S(2)}) collective-permute-start(f16[256,512]{1,0:T(8,128)(2,1)S(1)} %convert_element_type.26), channel_id=1, source_target_pairs={{2,0},{3,1},{4,2},{5,3},{6,4},{7,5},{8,6},{9,7},{10,8},{11,9},{12,... | collective-permute-start | bytes 786440 | tf_op jit(solution)/shard_map/ppermute | solution.py:22
  29.4 2.9 %collective-permute-start.3 = (f16[256,512]{1,0:T(8,128)(2,1)S(1)}, f16[256,512]{1,0:T(8,128)(2,1)S(1)}, u32[]{:S(2)}, u32[]{:S(2)}) collective-permute-start(f16[256,512]{1,0:T(8,128)(2,1)S(1)} %convert_element_type.28), channel_id=1, source_target_pairs={{0,1},{1,2},{2,3},{3,4},{4,5},{5,6},{6,7},{7,8},{8,9},{9,10},{10,1... | collective-permute-start | bytes 786440 | tf_op jit(solution)/shard_map/ppermute | solution.py:22
  32.3 0.7 %convert_element_type.30 = f16[256,512]{1,0:T(8,128)(2,1)} convert(f32[256,512]{1,0:T(8,128)S(1)} %get-tuple-element.14) | non-fusion elementwise | flops 131072 | bytes 786432 | tf_op jit(solution)/shard_map/convert_element_type | solution.py:84
  33.1 5.0 %collective-permute-start.4 = (f16[256,512]{1,0:T(8,128)(2,1)}, f16[256,512]{1,0:T(8,128)(2,1)S(1)}, u32[]{:S(2)}, u32[]{:S(2)}) collective-permute-start(f16[256,512]{1,0:T(8,128)(2,1)} %convert_element_type.30), channel_id=1, source_target_pairs={{1,0},{2,1},{3,2},{4,3},{5,4},{6,5},{7,6},{8,7},{9,8},{10,9},{11,1... | collective-permute-start | bytes 786440 | tf_op jit(solution)/shard_map/ppermute | solution.py:22
  38.1 0.0 all-to-all-done.rows_ref
  38.1 1.9 %collective-permute-start = (bf16[4,256,512]{2,1,0:T(8,128)(2,1)}, bf16[4,256,512]{2,1,0:T(8,128)(2,1)S(1)}, u32[]{:S(2)}, u32[]{:S(2)}) collective-permute-start(bf16[4,256,512]{2,1,0:T(8,128)(2,1)} %all-to-all-done.rows_ref), channel_id=1, source_target_pairs={{0,128},{128,0},{1,129},{129,1},{2,130},{130,2},{3,131},{131,3},{4... | collective-permute-start | bytes 3145736 | tf_op jit(solution)/shard_map/ppermute | solution.py:86
  40.0 0.0 copy-done.1
  40.1 1.7 %shard_map.65.before_ref = f32[256,512]{1,0:T(8,128)S(1)} custom-call(bf16[256,2048]{1,0:T(8,128)(2,1)S(1)} %copy-done.1, bf16[4,256,512]{2,1,0:T(8,128)(2,1)} %all-to-all-done.rows_ref, f32[256,512]{1,0:T(8,128)S(1)} %get-tuple-element.10.before_ref), custom_call_target="tpu_custom_call" | custom-call | flops 17179869184 | bytes 2097152 | tf_op jit(solution)/shard_map/pallas_call | solution.py:67
  41.7 0.0 copy-start.4
  41.7 0.0 copy-start.5
  41.7 1.1 %collective-permute-done.rows_ref = bf16[4,256,512]{2,1,0:T(8,128)(2,1)S(1)} collective-permute-done((bf16[4,256,512]{2,1,0:T(8,128)(2,1)}, bf16[4,256,512]{2,1,0:T(8,128)(2,1)S(1)}, u32[]{:S(2)}, u32[]{:S(2)}) %collective-permute-start) | collective-permute-done | bytes 1048608 | tf_op jit(solution)/shard_map/ppermute | solution.py:86
  42.9 0.4 shard_map.66
  43.3 0.0 collective-permute-done.1
  43.3 0.0 collective-permute-done.2
  43.4 1.1 %collective-permute-done.3 = f16[256,512]{1,0:T(8,128)(2,1)S(1)} collective-permute-done((f16[256,512]{1,0:T(8,128)(2,1)S(1)}, f16[256,512]{1,0:T(8,128)(2,1)S(1)}, u32[]{:S(2)}, u32[]{:S(2)}) %collective-permute-start.3) | collective-permute-done | bytes 262176 | tf_op jit(solution)/shard_map/ppermute | solution.py:22
  44.4 1.8 %collective-permute-done.4 = f16[256,512]{1,0:T(8,128)(2,1)S(1)} collective-permute-done((f16[256,512]{1,0:T(8,128)(2,1)}, f16[256,512]{1,0:T(8,128)(2,1)S(1)}, u32[]{:S(2)}, u32[]{:S(2)}) %collective-permute-start.4) | collective-permute-done | bytes 262176 | tf_op jit(solution)/shard_map/ppermute | solution.py:22
  46.3 0.0 copy-done.4
  46.3 0.0 copy-done.5
  46.3 1.0 %subtract_divide_fusion = f32[256,512]{1,0:T(8,128)} fusion(f32[256,512]{1,0:T(8,128)S(1)} %shard_map.66, f16[256,512]{1,0:T(8,128)(2,1)S(1)} %collective-permute-done.4, f16[256,512]{1,0:T(8,128)(2,1)S(1)} %collective-permute-done.3, f16[256,512]{1,0:T(8,128)(2,1)S(1)} %collective-permute-done.2, f16[256,512]{1,0:T(8,128)(2,1)S(1)} %collective-permute-done.1, ...), kind=kLoop, calls=%fused_computation | loop fusion | flops 1441792 | bytes 2100224 | tf_op jit(solution)/shard_map/div | solution.py:91
  (3 shorter events, 0.1 us)
Async XLA Ops:
  0.0 6.5 %copy-start.2 = (bf16[256,512]{1,0:T(8,128)(2,1)S(1)}, bf16[256,512]{1,0:T(8,128)(2,1)}, u32[]{:S(2)}) copy-start(bf16[256,512]{1,0:T(8,128)(2,1)} %amps_ref.1) | copy-start | bytes 786436
  0.0 6.5 %copy-start = (bf16[1,5,512,512]{3,2,1,0:T(8,128)(2,1)S(1)}, bf16[1,5,512,512]{3,2,1,0:T(8,128)(2,1)}, u32[]{:S(2)}) copy-start(bf16[1,5,512,512]{3,2,1,0:T(8,128)(2,1)} %blocks_ref.1) | copy-start | bytes 7864324
  0.0 6.5 %copy-start.3 = (s32[1,5]{1,0:T(1,128)S(1)}, s32[1,5]{1,0:T(1,128)}, u32[]{:S(2)}) copy-start(s32[1,5]{1,0:T(1,128)} %mask_ref.1) | copy-start | bytes 64
  2.2 35.9 %all-to-all-start = ((bf16[4,256,512]{2,1,0:T(8,128)(2,1)}), bf16[4,256,512]{2,1,0:T(8,128)(2,1)}, u32[]{:S(2)}, u32[]{:S(2)}) async-start(bf16[4,256,512]{2,1,0:T(8,128)(2,1)} %broadcast_in_dim.2), calls=%async_computation | async-start | bytes 2097152 | tf_op jit(solution)/shard_map/all_to_all | solution.py:81
  7.9 32.2 %copy-start.1 = (bf16[256,2048]{1,0:T(8,128)(2,1)S(1)}, bf16[256,2048]{1,0:T(8,128)(2,1)}, u32[]{:S(2)}) copy-start(bf16[256,2048]{1,0:T(8,128)(2,1)} %coupling_ref.3) | copy-start | bytes 3145732
  7.9 35.4 %collective-permute-start.1 = (f16[256,512]{1,0:T(8,128)(2,1)S(1)}, f16[256,512]{1,0:T(8,128)(2,1)S(1)}, u32[]{:S(2)}, u32[]{:S(2)}) collective-permute-start(f16[256,512]{1,0:T(8,128)(2,1)S(1)} %convert_element_type.24), channel_id=1, source_target_pairs={{0,2},{1,3},{2,4},{3,5},{4,6},{5,7},{6,8},{7,9},{8,10},{9,11},{10,... | collective-permute-start | bytes 786440 | tf_op jit(solution)/shard_map/ppermute | solution.py:22
  13.3 30.0 %collective-permute-start.2 = (f16[256,512]{1,0:T(8,128)(2,1)S(1)}, f16[256,512]{1,0:T(8,128)(2,1)S(1)}, u32[]{:S(2)}, u32[]{:S(2)}) collective-permute-start(f16[256,512]{1,0:T(8,128)(2,1)S(1)} %convert_element_type.26), channel_id=1, source_target_pairs={{2,0},{3,1},{4,2},{5,3},{6,4},{7,5},{8,6},{9,7},{10,8},{11,9},{12,... | collective-permute-start | bytes 786440 | tf_op jit(solution)/shard_map/ppermute | solution.py:22
  29.4 15.0 %collective-permute-start.3 = (f16[256,512]{1,0:T(8,128)(2,1)S(1)}, f16[256,512]{1,0:T(8,128)(2,1)S(1)}, u32[]{:S(2)}, u32[]{:S(2)}) collective-permute-start(f16[256,512]{1,0:T(8,128)(2,1)S(1)} %convert_element_type.28), channel_id=1, source_target_pairs={{0,1},{1,2},{2,3},{3,4},{4,5},{5,6},{6,7},{7,8},{8,9},{9,10},{10,1... | collective-permute-start | bytes 786440 | tf_op jit(solution)/shard_map/ppermute | solution.py:22
  33.1 13.2 %collective-permute-start.4 = (f16[256,512]{1,0:T(8,128)(2,1)}, f16[256,512]{1,0:T(8,128)(2,1)S(1)}, u32[]{:S(2)}, u32[]{:S(2)}) collective-permute-start(f16[256,512]{1,0:T(8,128)(2,1)} %convert_element_type.30), channel_id=1, source_target_pairs={{1,0},{2,1},{3,2},{4,3},{5,4},{6,5},{7,6},{8,7},{9,8},{10,9},{11,1... | collective-permute-start | bytes 786440 | tf_op jit(solution)/shard_map/ppermute | solution.py:22
  38.1 4.8 %collective-permute-start = (bf16[4,256,512]{2,1,0:T(8,128)(2,1)}, bf16[4,256,512]{2,1,0:T(8,128)(2,1)S(1)}, u32[]{:S(2)}, u32[]{:S(2)}) collective-permute-start(bf16[4,256,512]{2,1,0:T(8,128)(2,1)} %all-to-all-done.rows_ref), channel_id=1, source_target_pairs={{0,128},{128,0},{1,129},{129,1},{2,130},{130,2},{3,131},{131,3},{4... | collective-permute-start | bytes 3145736 | tf_op jit(solution)/shard_map/ppermute | solution.py:86
  41.7 4.5 %copy-start.4 = (f32[512]{0:T(512)S(1)}, f32[512]{0:T(512)}, u32[]{:S(2)}) copy-start(f32[512]{0:T(512)} %param.11) | copy-start | bytes 6148
  41.7 4.5 %copy-start.5 = (f32[256]{0:T(256)S(1)}, f32[256]{0:T(256)}, u32[]{:S(2)}) copy-start(f32[256]{0:T(256)} %param.10) | copy-start | bytes 3076
